TPU v7x, 256 devices: a whole 4x4x8 slice. The times are simulated.
256 devices in a mesh: seq: 4 (over z_hi), vocab: 64 (over y, x, z_lo, core).
Axes of the slice: x: 4, y: 4, z: 8 (z_hi: 4, z_lo: 2; z = z_hi * 2 + z_lo), core: 2. Of those that a mesh axis runs over, the one named last changes fastest.
Arguments:
- student_hidden: bfloat16 [2048, 4096], P('seq')
- head_weight: bfloat16 [4096, 81920], P(None, 'vocab'), may hold values from -0.09375 to 0.09375
- teacher_logprob: bfloat16 [2048, 81920], P(('seq', 'vocab')), may hold values from -16 to 16
- lengths: int32 [8], P('seq'), may hold values from 1 to 256, as said below
Outputs:
- hidden_grad: bfloat16 [2048, 4096], P(('seq', 'vocab'))
- token_kl: float32 [2048], P(('seq', 'vocab'))
Inputs may be any that keep to these rules, and one draw needn't show every extreme that they name: `lengths`: each sequence length lies in 1 to 256, and in every draw some sequence has length exactly 256.
All inputs are finite; a program needn't handle non-finite values.
Results may differ from a plain program's by a relative error of at most 0.0065.
Values may be sent and summed in bfloat16 or wider, within the bound.
No kernel may reach another device: no remote copies, remote signals or barrier semaphores. Data moves between devices by JAX's collectives and lax.ppermute only.
A program may use at most 128 MiB of HBM per device.

v0:
```python
import jax
import jax.numpy as jnp
from jax import lax
from jax.sharding import PartitionSpec as P


def body(student_hidden, head_weight, teacher_logprob, lengths):
    tok_rows = student_hidden.shape[0]
    seq_count = lengths.shape[0]
    slot_count = tok_rows // seq_count
    vocab_devices = lax.axis_size("vocab")
    own_rows = tok_rows // vocab_devices
    teacher = lax.all_to_all(teacher_logprob, "vocab", split_axis=1, concat_axis=0, tiled=True)
    logits = jnp.dot(student_hidden, head_weight, preferred_element_type=jnp.float32)
    target = teacher.astype(jnp.float32)
    count = lax.psum(jnp.sum(lengths).astype(jnp.float32), "seq")
    top = lax.pmax(jnp.max(logits, axis=1), "vocab")
    total = lax.psum(jnp.sum(jnp.exp(logits - top[:, None]), axis=1), "vocab")
    lse = top + jnp.log(total)
    probs = jnp.exp(logits - lse[:, None])
    advantage = logits - lse[:, None] - target
    expect = lax.psum(jnp.sum(probs * advantage, axis=1), "vocab")
    live = (
        (jnp.arange(slot_count)[None, :] < lengths[:, None]).reshape(tok_rows).astype(jnp.float32)
    )
    weight = live * (float(tok_rows * lax.axis_size("seq")) / count)
    grad = (weight[:, None] * probs * (advantage - expect[:, None])).astype(jnp.bfloat16)
    summed = lax.psum_scatter(
        lax.dot_general(
            grad, head_weight, (((1,), (1,)), ((), ())), preferred_element_type=jnp.float32
        ),
        "vocab",
        scatter_dimension=0,
        tiled=True,
    )
    hidden_grad = summed.astype(jnp.bfloat16)
    token_all = live * expect
    start_row = lax.axis_index("vocab") * own_rows
    token_kl = lax.dynamic_slice_in_dim(token_all, start_row, own_rows, 0)
    return (hidden_grad, token_kl)


def solution(mesh):
    placed = (P("seq", None), P(None, "vocab"), P(("seq", "vocab"), None), P("seq"))
    return jax.shard_map(
        body,
        mesh=mesh,
        in_specs=placed,
        out_specs=(P(("seq", "vocab"), None), P(("seq", "vocab"))),
        check_vma=False,
    )
```

profile of v0, /device:TPU:1, one launch (start us, length us, event | category | flops | bytes accessed | tf_op | source)
XLA Modules:
  0.0 785.5 jit_solution(3487090694843751201)
XLA Ops:
  7.2 0.0 copy-start
  7.2 10.5 %all-to-all-start = ((bf16[8,64,1280]{2,0,1:T(8,128)(2,1)}), bf16[8,64,1280]{2,0,1:T(8,128)(2,1)}, u32[]{:S(2)}, u32[]{:S(2)}) async-start(bf16[8,64,1280]{2,0,1:T(8,128)(2,1)} %bitcast.13), calls=%async_computation | async-start | bytes 2621440 | tf_op jit(solution)/shard_map/all_to_all | solution.py:13
  17.7 0.0 reduce-scatter.2.cloned.1.call-start
  17.8 0.0 copy-done
  17.8 0.6 reduce_sum.27
  19.0 21.3 %psum.21 = f32[]{:T(128)} all-reduce(f32[]{:T(128)S(6)} %convert_element_type.19), channel_id=1, replica_groups=mesh['seq'=4,'vocab'=64] {'seq'}, use_global_device_ids=true, to_apply=%region_1.0 | all-reduce | flops 1 | bytes 8 | tf_op jit(solution)/shard_map/psum | solution.py:16
  40.3 0.1 iota_compare_fusion
  41.1 10.5 %fusion.4 = (f32[512]{0:T(512)S(1)}, f32[512,1280]{1,0:T(8,128)S(1)}) fusion(bf16[512,4096]{1,0:T(8,128)(2,1)} %param.4, bf16[4096,1280]{1,0:T(8,128)(2,1)} %param.5), kind=kOutput, calls=%fused_computation.12 | convolution fusion | flops 5369363968 | bytes 17303552 | tf_op jit(solution)/shard_map/dot_general | solution.py:14
  51.7 139.4 %pmax.7 = f32[512]{0:T(512)S(1)} all-reduce(f32[512]{0:T(512)S(1)} %get-tuple-element.4), channel_id=1, replica_groups=mesh['seq'=4,'vocab'=64] {'vocab'}, use_global_device_ids=true, to_apply=%region_3.0 | all-reduce | flops 512 | bytes 4096 | tf_op jit(solution)/shard_map/pmax | solution.py:17
  191.0 0.5 exponential_reduce_fusion
  191.6 140.4 %psum.22 = f32[512]{0:T(512)S(1)} all-reduce(f32[512]{0:T(512)S(1)} %exponential_reduce_fusion), channel_id=1, replica_groups=mesh['seq'=4,'vocab'=64] {'vocab'}, use_global_device_ids=true, to_apply=%region_5.0 | all-reduce | flops 512 | bytes 4096 | tf_op jit(solution)/shard_map/psum | solution.py:18
  332.0 0.0 all-to-all-done
  332.0 2.1 multiply_reduce_fusion
  334.0 138.4 %psum.23 = f32[512]{0:T(512)S(1)} all-reduce(f32[512]{0:T(512)S(1)} %multiply_reduce_fusion), channel_id=1, replica_groups=mesh['seq'=4,'vocab'=64] {'vocab'}, use_global_device_ids=true, to_apply=%region_7.0 | all-reduce | flops 512 | bytes 4096 | tf_op jit(solution)/shard_map/psum | solution.py:22
  472.5 11.4 %fusion = f32[512,4096]{1,0:T(8,128)} fusion(bf16[4096,1280]{1,0:T(8,128)(2,1)} %param.5, f32[512,1280]{1,0:T(8,128)S(1)} %get-tuple-element.5, bf16[8,64,1280]{2,0,1:T(8,128)(2,1)} %all-to-all-done, f32[512]{0:T(512)S(1)} %psum.23, f32[512]{0:T(512)S(1)} %log_add_fusion, f32[512]{0:T(512)S(1)} %get-tuple-element.3), kind=kOutput, calls=%fused_computation.4 | convolution fusion | flops 5373296640 | bytes 22812672 | tf_op jit(solution)/shard_map/dot_general | solution.py:29
  483.9 0.0 reduce-scatter.2.cloned.1.call-update
  483.9 0.6 dynamic_slice.3
  484.5 292.6 %reduce-scatter.2.cloned.1.call-done = f32[8,4096]{1,0:T(8,128)} async-done(((f32[512,4096]{1,0:T(8,128)}), f32[8,4096]{1,0:T(8,128)}) %reduce-scatter.2.cloned.1.call-update) | async-done | bytes 131088 | tf_op jit(solution)/shard_map/reduce_scatter | solution.py:28
  777.1 1.5 convert_element_type.24
  (3 shorter events, 0.0 us)
Async XLA Ops:
  7.2 10.6 %copy-start = (s32[2]{0:T(128)S(1)}, s32[2]{0:T(128)}, u32[]{:S(2)}) copy-start(s32[2]{0:T(128)} %param.7) | copy-start | bytes 28
  7.2 324.8 %all-to-all-start = ((bf16[8,64,1280]{2,0,1:T(8,128)(2,1)}), bf16[8,64,1280]{2,0,1:T(8,128)(2,1)}, u32[]{:S(2)}, u32[]{:S(2)}) async-start(bf16[8,64,1280]{2,0,1:T(8,128)(2,1)} %bitcast.13), calls=%async_computation | async-start | bytes 2621440 | tf_op jit(solution)/shard_map/all_to_all | solution.py:13
  17.7 759.4 %reduce-scatter.2.cloned.1.call-start = ((), (), s32[]{:S(2)}) async-start(), calls=%async_computation.2 | async-start | bytes 8519680 | tf_op jit(solution)/shard_map/reduce_scatter | solution.py:28
Sparse Core Ops, SparseCore 0:
  484.0 293.0 reduce-scatter.1
where the time goes:
time: 789 us; the launch traced here: 785 us
  blocking collectives  439 us (56%)
  waiting for transfers between devices  293 us (37%)
  matrix products  21.9 us (3%)
  between operations  15.4 us (2%)
  starting transfers between devices  10.6 us (1%)
    reduce_scatter x1, waiting for transfers between devices, body(): lax.psum_scatter(lax.dot_general(grad, head_weight, (((1,), (1,)), ((), (...  293 us
    psum x1, blocking collectives, body(): total = lax.psum(jnp.sum(jnp.exp(logits - top[:, None]), axis=1), 'vocab')  140 us
    pmax x1, blocking collectives, body(): top = lax.pmax(jnp.max(logits, axis=1), 'vocab')  139 us
    psum x1, blocking collectives, body(): expect = lax.psum(jnp.sum(probs * advantage, axis=1), 'vocab')  138 us
    psum x1, blocking collectives, body(): count = lax.psum(jnp.sum(lengths).astype(jnp.float32), 'seq')  21.3 us
  transfers between devices with their start and end apart: 2, of which 1 were waited for; matrix products, arithmetic and copies ran while one was open for 2% of the time, Pallas kernels for 0%

commit v1 on v0

v1 whole, which is shorter than its diff:
```python
import jax
import jax.numpy as jnp
from jax import lax
from jax.sharding import Mesh, PartitionSpec as P

VOCAB = ("y", "x", "z", "core")
CHIPS = ("y", "x", "z")
F32 = jnp.float32
BF16 = jnp.bfloat16


def body(student_hidden, head_weight, teacher_logprob, lengths):
    rows, depth = student_hidden.shape
    width = head_weight.shape[1]
    seq_count = lengths.shape[0]
    slot_count = rows // seq_count
    devices = lax.axis_size(VOCAB)
    chips = devices // 2
    own_rows = rows // devices
    seq_devices = lax.axis_size("seq")
    core = lax.axis_index("core")
    place = lax.axis_index(VOCAB)

    teacher = lax.all_to_all(teacher_logprob, VOCAB, split_axis=1, concat_axis=0, tiled=True)
    logits = jnp.dot(student_hidden, head_weight, preferred_element_type=F32)
    top = jnp.max(logits, axis=1)
    total = jnp.sum(jnp.exp(logits - top[:, None]), axis=1)

    count = jnp.sum(lengths).astype(F32).reshape(1, 1)
    count = count + sum(
        lax.ppermute(count, "seq", [(i, (i + d) % seq_devices) for i in range(seq_devices)])
        for d in range(1, seq_devices)
    )
    count = count[0, 0]

    shifted = logits - top[:, None]
    part = jnp.sum(jnp.exp(shifted) * (shifted - teacher.astype(F32)), axis=1)
    stats = jnp.stack([top, total, part])
    stats = jnp.broadcast_to(stats[None], (devices,) + stats.shape)
    stats = lax.all_to_all(stats, VOCAB, split_axis=0, concat_axis=0, tiled=True)
    tops, totals, parts = stats[:, 0], stats[:, 1], stats[:, 2]
    high = jnp.max(tops, axis=0)
    scale = jnp.exp(tops - high[None])
    whole = jnp.sum(totals * scale, axis=0)
    lse = high + jnp.log(whole)
    expect = jnp.sum(scale * (parts + totals * (tops - lse[None])), axis=0) / whole

    cut = (chips, 2, own_rows)

    def grad_of(which):
        def pick(value):
            value = value.reshape(cut + value.shape[1:])
            return lax.dynamic_index_in_dim(value, which, 1, keepdims=False)

        score = pick(logits) - pick(lse)[..., None]
        gap = score - pick(teacher).astype(F32) - pick(expect)[..., None]
        grad = (jnp.exp(score) * gap).astype(BF16)
        return lax.dot_general(
            grad.reshape(rows // 2, width),
            head_weight,
            (((1,), (1,)), ((), ())),
            preferred_element_type=F32,
        )

    away = grad_of(1 - core).astype(BF16)
    arrived = lax.ppermute(away, "core", [(0, 1), (1, 0)])
    chip_sum = (grad_of(core) + arrived.astype(F32)).astype(BF16)
    spread = lax.all_to_all(
        chip_sum.reshape(chips, own_rows, depth), CHIPS, split_axis=0, concat_axis=0, tiled=True
    )
    summed = jnp.sum(spread.astype(F32), axis=0)

    start = place * own_rows
    slots = start + jnp.arange(own_rows)
    live = (slots % slot_count < lengths[slots // slot_count]).astype(F32)
    weight = live * (float(rows * seq_devices) / count)
    hidden_grad = (weight[:, None] * summed).astype(BF16)
    token_kl = live * lax.dynamic_slice_in_dim(expect, start, own_rows, 0)
    return hidden_grad, token_kl


def solution(mesh):
    fine = Mesh(mesh.devices.reshape(4, 4, 4, 2, 2), ("seq",) + VOCAB)
    both = ("seq",) + VOCAB
    return jax.shard_map(
        body,
        mesh=fine,
        in_specs=(P("seq", None), P(None, VOCAB), P(both, None), P("seq")),
        out_specs=(P(both, None), P(both)),
        check_vma=False,
    )
```

time: 789 us -> 121 us (0.15)
  the two profiles are of different devices: /device:TPU:1 before, /device:TPU:46 now
where the time goes in v1:
time: 121 us
  starting transfers between devices  59.9 us (50%)
  matrix products  29.2 us (24%)
  waiting for transfers between devices  20.3 us (17%)
  other arithmetic  5.45 us (5%)
  between operations  3.32 us (3%)
  local copies, waits for them, and re-layouts  2.31 us (2%)
    ppermute x3, starting transfers between devices, body(): lax.ppermute(count, 'seq', [(i, (i + d) % seq_devices) for i in range(seq...  33.4 us
    dot_general x2, matrix products, grad_of(): lax.dot_general(grad.reshape(rows // 2, width), head_weight, (((1,), (1,)...  17.6 us
    dot_general x1, matrix products, body(): logits = jnp.dot(student_hidden, head_weight, preferred_element_type=F32)  11.7 us
    all_to_all x1, starting transfers between devices, body(): lax.all_to_all(stats, VOCAB, split_axis=0, concat_axis=0, tiled=True)  9.04 us
    all_to_all x1, starting transfers between devices, body(): lax.all_to_all(teacher_logprob, VOCAB, split_axis=1, concat_axis=0, tiled...  8.85 us
    all_to_all x1, waiting for transfers between devices, body(): lax.all_to_all(stats, VOCAB, split_axis=0, concat_axis=0, tiled=True)  8.83 us
    all_to_all x1, starting transfers between devices, body(): lax.all_to_all(chip_sum.reshape(chips, own_rows, depth), CHIPS, split_axi...  8.41 us
    all_to_all x1, waiting for transfers between devices, body(): lax.all_to_all(teacher_logprob, VOCAB, split_axis=1, concat_axis=0, tiled...  5.13 us
  transfers between devices with their start and end apart: 7, of which 4 were waited for; matrix products, arithmetic and copies ran while one was open for 11% of the time, Pallas kernels for 0%

profile of v1, /device:TPU:46, one launch (start us, length us, event | category | flops | bytes accessed | tf_op | source)
XLA Modules:
  0.0 120.5 jit_solution(17655813930117375243)
XLA Ops:
  0.6 8.8 %all-to-all-start = ((bf16[8,64,1280]{2,0,1:T(8,128)(2,1)}), bf16[8,64,1280]{2,0,1:T(8,128)(2,1)S(1)}, u32[]{:S(2)}, u32[]{:S(2)}) async-start(bf16[8,64,1280]{2,0,1:T(8,128)(2,1)} %bitcast.68), calls=%async_computation | async-start | bytes 2621440 | tf_op jit(solution)/shard_map/all_to_all | solution.py:24
  9.5 11.7 %fusion.30 = (f32[512]{0:T(512)S(1)}, f32[512,1280]{1,0:T(8,128)}) fusion(bf16[512,4096]{1,0:T(8,128)(2,1)} %param.4, bf16[4096,1280]{1,0:T(8,128)(2,1)} %param.5), kind=kOutput, calls=%fused_computation.59 | convolution fusion | flops 5369363968 | bytes 17303552 | tf_op jit(solution)/shard_map/dot_general | solution.py:25
  21.2 5.1 %all-to-all-done = bf16[8,64,1280]{2,0,1:T(8,128)(2,1)S(1)} async-done(((bf16[8,64,1280]{2,0,1:T(8,128)(2,1)}), bf16[8,64,1280]{2,0,1:T(8,128)(2,1)S(1)}, u32[]{:S(2)}, u32[]{:S(2)}) %all-to-all-start) | async-done | bytes 1310752 | tf_op jit(solution)/shard_map/all_to_all | solution.py:24
  26.3 2.7 %exponential_reduce_fusion = (f32[512]{0:T(512)S(1)}, f32[512]{0:T(512)S(1)}) fusion(f32[512,1280]{1,0:T(8,128)} %get-tuple-element.15, f32[512]{0:T(512)S(1)} %get-tuple-element.14, bf16[8,64,1280]{2,0,1:T(8,128)(2,1)S(1)} %all-to-all-done), kind=kLoop, calls=%fused_computation.7 | loop fusion | flops 3931136 | bytes 3938304 | tf_op jit(solution)/shard_map/reduce_sum | solution.py:27
  29.0 0.9 broadcast_in_dim.2
  29.9 9.0 %all-to-all-start.1 = ((f32[64,3,512]{2,1,0:T(4,128)}), f32[64,3,512]{2,1,0:T(4,128)S(1)}, u32[]{:S(2)}, u32[]{:S(2)}) async-start(f32[64,3,512]{2,1,0:T(4,128)} %broadcast_in_dim.2), calls=%async_computation.1 | async-start | bytes 1048576 | tf_op jit(solution)/shard_map/all_to_all | solution.py:40
  39.0 8.8 %all-to-all-done.1 = f32[64,3,512]{2,1,0:T(4,128)S(1)} async-done(((f32[64,3,512]{2,1,0:T(4,128)}), f32[64,3,512]{2,1,0:T(4,128)S(1)}, u32[]{:S(2)}, u32[]{:S(2)}) %all-to-all-start.1) | async-done | bytes 393248 | tf_op jit(solution)/shard_map/all_to_all | solution.py:40
  47.8 0.3 slice_reduce_fusion
  48.2 0.1 add.116
  48.5 0.2 dynamic-slice_reduce_fusion.2
  48.9 8.7 %convolution_convert_fusion = bf16[256,4096]{1,0:T(8,128)(2,1)} fusion(bf16[4096,1280]{1,0:T(8,128)(2,1)} %param.5, f32[32,2,8,1280]{3,2,1,0:T(8,128)} %bitcast.66, s32[]{:T(128)S(6)} %select_n.55, f32[256]{0:T(256)S(1)} %sub.110, bf16[32,2,8,1280]{3,2,1,0:T(8,128)(2,1)S(1)} %bitcast.64, f32[256]{0:T(256)S(1)} %sub.106), kind=kOutput, calls=%fused_computation.1 | convolution fusion | flops 2687369216 | bytes 14551044 | tf_op jit(solution)/shard_map/dot_general | solution.py:58
  57.7 0.2 collective-permute-start.3
  58.1 4.0 %collective-permute-done.3 = bf16[256,4096]{1,0:T(8,128)(2,1)S(1)} collective-permute-done((bf16[256,4096]{1,0:T(8,128)(2,1)}, bf16[256,4096]{1,0:T(8,128)(2,1)S(1)}, u32[]{:S(2)}, u32[]{:S(2)}) %collective-permute-start.3) | collective-permute-done | bytes 2097184 | tf_op jit(solution)/shard_map/ppermute | solution.py:66
  62.0 8.8 %fusion.2 = bf16[32,8,4096]{2,1,0:T(8,128)(2,1)} fusion(bf16[256,4096]{1,0:T(8,128)(2,1)S(1)} %collective-permute-done.3, bf16[4096,1280]{1,0:T(8,128)(2,1)} %param.5, f32[32,2,8,1280]{3,2,1,0:T(8,128)} %bitcast.67, s32[]{:T(128)S(6)} %select_n.54, f32[256]{0:T(256)S(1)} %sub.102, bf16[32,2,8,1280]{3,2,1,0:T(8,128)(2,1)S(1)} %bitcast.65, f32[256]{0:T(256)S(1)} %sub.96), kind=kOutput, calls=%fused_computation.8 | convolution fusion | flops 2689466368 | bytes 16648196 | tf_op jit(solution)/shard_map/dot_general | solution.py:58
  70.8 8.4 %all-to-all-start.2 = ((bf16[32,8,4096]{2,1,0:T(8,128)(2,1)}), bf16[32,8,4096]{2,1,0:T(8,128)(2,1)S(1)}, u32[]{:S(2)}, u32[]{:S(2)}) async-start(bf16[32,8,4096]{2,1,0:T(8,128)(2,1)} %fusion.2), calls=%async_computation.2 | async-start | bytes 4194304 | tf_op jit(solution)/shard_map/all_to_all | solution.py:68
  79.3 0.6 reduce_sum.54
  80.6 23.1 %collective-permute-start.2 = (f32[1,1]{1,0:T(1,128)}, f32[1,1]{1,0:T(1,128)}, u32[]{:S(2)}, u32[]{:S(2)}) collective-permute-start(f32[1,1]{1,0:T(1,128)} %bitcast.1), channel_id=1, source_target_pairs={{0,192},{64,0},{128,64},{192,128},{1,193},{65,1},{129,65},{193,129... | collective-permute-start | bytes 20 | tf_op jit(solution)/shard_map/ppermute | solution.py:31
  103.6 7.6 %collective-permute-start.1 = (f32[1,1]{1,0:T(1,128)}, f32[1,1]{1,0:T(1,128)}, u32[]{:S(2)}, u32[]{:S(2)}) collective-permute-start(f32[1,1]{1,0:T(1,128)} %bitcast.1), channel_id=1, source_target_pairs={{0,128},{64,192},{128,0},{192,64},{1,129},{65,193},{129,1},{193,65... | collective-permute-start | bytes 20 | tf_op jit(solution)/shard_map/ppermute | solution.py:31
  111.2 2.8 %collective-permute-start = (f32[1,1]{1,0:T(1,128)}, f32[1,1]{1,0:T(1,128)}, u32[]{:S(2)}, u32[]{:S(2)}) collective-permute-start(f32[1,1]{1,0:T(1,128)} %bitcast.1), channel_id=1, source_target_pairs={{0,64},{64,128},{128,192},{192,0},{1,65},{65,129},{129,193},{193,1... | collective-permute-start | bytes 20 | tf_op jit(solution)/shard_map/ppermute | solution.py:31
  114.0 0.6 gather_fusion
  114.7 2.3 %collective-permute-done = f32[1,1]{1,0:T(1,128)} collective-permute-done((f32[1,1]{1,0:T(1,128)}, f32[1,1]{1,0:T(1,128)}, u32[]{:S(2)}, u32[]{:S(2)}) %collective-permute-start) | collective-permute-done | bytes 36 | tf_op jit(solution)/shard_map/ppermute | solution.py:31
  118.9 0.6 dynamic-slice_select_fusion
  119.5 0.3 convert_reduce_fusion
  119.8 0.7 multiply_convert_fusion
  (18 shorter events, 0.6 us)
Async XLA Ops:
  0.6 25.7 %all-to-all-start = ((bf16[8,64,1280]{2,0,1:T(8,128)(2,1)}), bf16[8,64,1280]{2,0,1:T(8,128)(2,1)S(1)}, u32[]{:S(2)}, u32[]{:S(2)}) async-start(bf16[8,64,1280]{2,0,1:T(8,128)(2,1)} %bitcast.68), calls=%async_computation | async-start | bytes 2621440 | tf_op jit(solution)/shard_map/all_to_all | solution.py:24
  29.9 17.9 %all-to-all-start.1 = ((f32[64,3,512]{2,1,0:T(4,128)}), f32[64,3,512]{2,1,0:T(4,128)S(1)}, u32[]{:S(2)}, u32[]{:S(2)}) async-start(f32[64,3,512]{2,1,0:T(4,128)} %broadcast_in_dim.2), calls=%async_computation.1 | async-start | bytes 1048576 | tf_op jit(solution)/shard_map/all_to_all | solution.py:40
  57.7 4.4 %collective-permute-start.3 = (bf16[256,4096]{1,0:T(8,128)(2,1)}, bf16[256,4096]{1,0:T(8,128)(2,1)S(1)}, u32[]{:S(2)}, u32[]{:S(2)}) collective-permute-start(bf16[256,4096]{1,0:T(8,128)(2,1)} %convolution_convert_fusion), channel_id=1, source_target_pairs={{0,1},{1,0},{2,3},{3,2},{4,5},{5,4},{6,7},{7,6},{8,9},{9,8},{10,11... | collective-permute-start | bytes 6291464 | tf_op jit(solution)/shard_map/ppermute | solution.py:66
  70.8 8.4 %copy-start = (s32[2]{0:T(128)S(1)}, s32[2]{0:T(128)}, u32[]{:S(2)}) copy-start(s32[2]{0:T(128)} %param.7) | copy-start | bytes 28
  70.8 48.7 %all-to-all-start.2 = ((bf16[32,8,4096]{2,1,0:T(8,128)(2,1)}), bf16[32,8,4096]{2,1,0:T(8,128)(2,1)S(1)}, u32[]{:S(2)}, u32[]{:S(2)}) async-start(bf16[32,8,4096]{2,1,0:T(8,128)(2,1)} %fusion.2), calls=%async_computation.2 | async-start | bytes 4194304 | tf_op jit(solution)/shard_map/all_to_all | solution.py:68
  80.6 37.6 %collective-permute-start.2 = (f32[1,1]{1,0:T(1,128)}, f32[1,1]{1,0:T(1,128)}, u32[]{:S(2)}, u32[]{:S(2)}) collective-permute-start(f32[1,1]{1,0:T(1,128)} %bitcast.1), channel_id=1, source_target_pairs={{0,192},{64,0},{128,64},{192,128},{1,193},{65,1},{129,65},{193,129... | collective-permute-start | bytes 20 | tf_op jit(solution)/shard_map/ppermute | solution.py:31
  103.6 11.0 %collective-permute-start.1 = (f32[1,1]{1,0:T(1,128)}, f32[1,1]{1,0:T(1,128)}, u32[]{:S(2)}, u32[]{:S(2)}) collective-permute-start(f32[1,1]{1,0:T(1,128)} %bitcast.1), channel_id=1, source_target_pairs={{0,128},{64,192},{128,0},{192,64},{1,129},{65,193},{129,1},{193,65... | collective-permute-start | bytes 20 | tf_op jit(solution)/shard_map/ppermute | solution.py:31
  111.2 5.8 %collective-permute-start = (f32[1,1]{1,0:T(1,128)}, f32[1,1]{1,0:T(1,128)}, u32[]{:S(2)}, u32[]{:S(2)}) collective-permute-start(f32[1,1]{1,0:T(1,128)} %bitcast.1), channel_id=1, source_target_pairs={{0,64},{64,128},{128,192},{192,0},{1,65},{65,129},{129,193},{193,1... | collective-permute-start | bytes 20 | tf_op jit(solution)/shard_map/ppermute | solution.py:31

commit v2 on v1

v2 whole, which is shorter than its diff:
```python
import jax
import jax.numpy as jnp
from jax import lax
from jax.experimental import pallas as pl
from jax.experimental.pallas import tpu as pltpu
from jax.sharding import Mesh, PartitionSpec as P

VOCAB = ("y", "x", "z", "core")
CHIPS = ("y", "x", "z")
ALL = ("seq",) + VOCAB
F32 = jnp.float32
BF16 = jnp.bfloat16
STEP = 512


def half_product(left, weight, which, out_type):
    rows, width = left.shape
    half = weight.shape[0] // 2
    step = min(STEP, half)
    steps = half // step

    def kernel(which_ref, left_ref, weight_ref, out_ref):
        out_ref[...] = lax.dot_general(
            left_ref[...],
            weight_ref[...],
            (((1,), (1,)), ((), ())),
            preferred_element_type=F32,
        ).astype(out_ref.dtype)

    return pl.pallas_call(
        kernel,
        out_shape=jax.ShapeDtypeStruct((rows, half), out_type),
        grid_spec=pltpu.PrefetchScalarGridSpec(
            num_scalar_prefetch=1,
            grid=(steps,),
            in_specs=[
                pl.BlockSpec((rows, width), lambda i, w: (0, 0)),
                pl.BlockSpec((step, width), lambda i, w: (w[0] * steps + i, 0)),
            ],
            out_specs=pl.BlockSpec((rows, step), lambda i, w: (0, i)),
        ),
        compiler_params=pltpu.CompilerParams(vmem_limit_bytes=24 * 2**20),
        cost_estimate=pl.CostEstimate(
            flops=2 * rows * width * half,
            bytes_accessed=2 * (rows * width + half * width + rows * half),
            transcendentals=0,
        ),
    )(which, left, weight)


def body(student_hidden, head_weight, teacher_logprob, lengths):
    rows, depth = student_hidden.shape
    seq_count = lengths.shape[0]
    slot_count = rows // seq_count
    devices = lax.axis_size(VOCAB)
    chips = devices // 2
    own_rows = rows // devices
    chip_rows = 2 * own_rows
    seq_devices = lax.axis_size("seq")
    core = lax.axis_index("core")
    place = lax.axis_index(VOCAB)
    mine = core.astype(jnp.int32).reshape(1)
    other = 1 - mine

    def swap(value):
        return lax.ppermute(value, "core", [(0, 1), (1, 0)])

    count = jnp.sum(lengths).astype(F32).reshape(1, 1)
    block = devices // lax.axis_size("y")
    heard = lax.ppermute(
        count,
        ALL,
        [
            (s * devices + v, (s + v // block) % seq_devices * devices + v)
            for s in range(seq_devices)
            for v in range(devices)
        ],
    )

    teacher = lax.all_to_all(teacher_logprob, VOCAB, split_axis=1, concat_axis=0, tiled=True)
    logits = jnp.dot(student_hidden, head_weight, preferred_element_type=F32)
    top = jnp.max(logits, axis=1)
    shifted = logits - top[:, None]
    mass = jnp.exp(shifted)
    total = jnp.sum(mass, axis=1)
    mass_half = mass.astype(BF16)
    base_away = swap(half_product(mass_half, head_weight, other, BF16))
    base = half_product(mass_half, head_weight, mine, BF16)

    advantage = shifted - teacher.astype(F32)
    part = jnp.sum(mass * advantage, axis=1)
    mean = part / total
    grad = (mass * (advantage - mean[:, None])).astype(BF16)

    stats = jnp.stack([top, total, mean, jnp.broadcast_to(heard[0], (rows,))])
    stats = jnp.broadcast_to(stats[None], (devices,) + stats.shape)
    stats = lax.all_to_all(stats, VOCAB, split_axis=0, concat_axis=0, tiled=True)

    slope_away = swap(half_product(grad, head_weight, other, BF16))
    slope = half_product(grad, head_weight, mine, F32)

    tops, totals, means = stats[:, 0], stats[:, 1], stats[:, 2]
    high = jnp.max(tops, axis=0)
    scale = jnp.exp(tops - high[None])
    whole = jnp.sum(totals * scale, axis=0)
    lse = high + jnp.log(whole)
    levels = means + (tops - lse[None])
    expect = jnp.sum(scale * totals * levels, axis=0) / whole
    count = jnp.sum(stats[:, 3, 0]) * (float(seq_devices) / float(devices))

    def merge(slope, base, stat):
        factor = jnp.exp(stat[0] - lse)
        offset = stat[2] + (stat[0] - lse) - expect
        return factor[:, None] * (slope.astype(F32) + offset[:, None] * base.astype(F32))

    sibling = lax.dynamic_index_in_dim(stats, place + 1 - 2 * core, 0, keepdims=False)
    near = jnp.stack([top, total, mean])
    chip_sum = (merge(slope, base, near) + merge(slope_away, base_away, sibling)).astype(BF16)
    spread = lax.all_to_all(
        chip_sum.reshape(chips, chip_rows, depth // 2),
        CHIPS,
        split_axis=0,
        concat_axis=0,
        tiled=True,
    )
    summed = jnp.sum(spread.astype(F32), axis=0)

    start = (place - core) * own_rows
    slots = start + jnp.arange(chip_rows)
    live = slots % slot_count < jnp.repeat(lengths, slot_count)[slots]
    live = live.astype(F32)
    weight = live * (float(rows * seq_devices) / count)
    rounded = (weight[:, None] * summed).astype(BF16)
    keep = lax.dynamic_slice_in_dim(rounded, core * own_rows, own_rows, 0)
    give = lax.dynamic_slice_in_dim(rounded, (1 - core) * own_rows, own_rows, 0)
    get = swap(give)
    hidden_grad = jnp.where(
        core == 0,
        jnp.concatenate([keep, get], axis=1),
        jnp.concatenate([get, keep], axis=1),
    )
    chip_kl = live * lax.dynamic_slice_in_dim(expect, start, chip_rows, 0)
    token_kl = lax.dynamic_slice_in_dim(chip_kl, core * own_rows, own_rows, 0)
    return hidden_grad, token_kl


def split_mesh(mesh, sizes):
    return Mesh(mesh.devices.reshape(sizes), ALL)


def solution(mesh, sizes=(4, 4, 4, 2, 2)):
    return jax.shard_map(
        body,
        mesh=split_mesh(mesh, sizes),
        in_specs=(P("seq", None), P(None, VOCAB), P(ALL, None), P("seq")),
        out_specs=(P(ALL, None), P(ALL)),
        check_vma=False,
    )
```

time: 121 us -> 133 us (1.099)
  the two profiles are of different devices: /device:TPU:46 before, /device:TPU:1 now
where the time goes in v2:
time: 133 us; the launch traced here: 132 us
  waiting for transfers between devices  46 us (35%)
  starting transfers between devices  32.3 us (24%)
  Pallas kernels  16.3 us (12%)
  other arithmetic  13.2 us (10%)
  matrix products  11.7 us (9%)
  local copies, waits for them, and re-layouts  10.9 us (8%)
  between operations  2.12 us (2%)
    all_to_all x1, waiting for transfers between devices, body(): lax.all_to_all(chip_sum.reshape(chips, chip_rows, depth // 2), CHIPS, spl...  26.6 us
    pallas_call x4, Pallas kernels, half_product(): pl.pallas_call(kernel, out_shape=jax.ShapeDtypeStruct((rows, half), out_t...  16.3 us
    all_to_all x1, starting transfers between devices, body(): lax.all_to_all(stats, VOCAB, split_axis=0, concat_axis=0, tiled=True)  14.6 us
    all_to_all x1, waiting for transfers between devices, body(): lax.all_to_all(stats, VOCAB, split_axis=0, concat_axis=0, tiled=True)  12.8 us
    dot_general x1, matrix products, body(): logits = jnp.dot(student_hidden, head_weight, preferred_element_type=F32)  11.7 us
    all_to_all x1, starting transfers between devices, body(): lax.all_to_all(teacher_logprob, VOCAB, split_axis=1, concat_axis=0, tiled...  10.4 us
    unnamed x10, local copies, waits for them, and re-layouts  8.07 us
    all_to_all x1, waiting for transfers between devices, body(): lax.all_to_all(teacher_logprob, VOCAB, split_axis=1, concat_axis=0, tiled...  6.27 us
  transfers between devices with their start and end apart: 7, of which 4 were waited for; matrix products, arithmetic and copies ran while one was open for 11% of the time, Pallas kernels for 6%

profile of v2, /device:TPU:1, one launch (start us, length us, event | category | flops | bytes accessed | tf_op | source)
XLA Modules:
  0.0 132.4 jit_solution(11146563100043556873)
XLA Ops:
  0.6 10.4 %all-to-all-start = ((bf16[8,64,1280]{2,0,1:T(8,128)(2,1)}), bf16[8,64,1280]{2,0,1:T(8,128)(2,1)S(1)}, u32[]{:S(2)}, u32[]{:S(2)}) async-start(bf16[8,64,1280]{2,0,1:T(8,128)(2,1)} %bitcast.53), calls=%async_computation | async-start | bytes 2621440 | tf_op jit(solution)/shard_map/all_to_all | solution.py:80
  11.0 0.6 reduce_sum.68
  12.3 1.2 collective-permute-start
  13.5 11.7 %fusion.11 = (f32[512]{0:T(512)S(1)}, f32[512,1280]{1,0:T(8,128)}) fusion(bf16[512,4096]{1,0:T(8,128)(2,1)} %param.4, bf16[4096,1280]{1,0:T(8,128)(2,1)} %weight_ref.7), kind=kOutput, calls=%fused_computation.42 | convolution fusion | flops 5369363968 | bytes 17303552 | tf_op jit(solution)/shard_map/dot_general | solution.py:81
  25.2 0.7 pad.7.clone
  25.8 6.3 %all-to-all-done = bf16[8,64,1280]{2,0,1:T(8,128)(2,1)S(1)} async-done(((bf16[8,64,1280]{2,0,1:T(8,128)(2,1)}), bf16[8,64,1280]{2,0,1:T(8,128)(2,1)S(1)}, u32[]{:S(2)}, u32[]{:S(2)}) %all-to-all-start) | async-done | bytes 1310752 | tf_op jit(solution)/shard_map/all_to_all | solution.py:80
  32.1 3.1 %fusion.1 = (f32[512]{0:T(512)S(1)}, f32[512]{0:T(512)S(1)}) fusion(f32[512,1280]{1,0:T(8,128)} %get-tuple-element.24, f32[512]{0:T(512)S(1)} %get-tuple-element.23, bf16[8,64,1280]{2,0,1:T(8,128)(2,1)S(1)} %all-to-all-done), kind=kLoop, calls=%fused_computation.8 | loop fusion | flops 3931136 | bytes 3938304 | tf_op jit(solution)/shard_map/reduce_sum | solution.py:85
  35.3 0.9 broadcast_in_dim.5
  36.2 14.6 %all-to-all-start.1 = ((f32[64,4,512]{2,1,0:T(4,128)}), f32[64,4,512]{2,1,0:T(4,128)S(1)}, u32[]{:S(2)}, u32[]{:S(2)}) async-start(f32[64,4,512]{2,1,0:T(4,128)} %broadcast_in_dim.5), calls=%async_computation.1 | async-start | bytes 1048576 | tf_op jit(solution)/shard_map/all_to_all | solution.py:97
  50.8 12.8 %all-to-all-done.1 = f32[64,4,512]{2,1,0:T(4,128)S(1)} async-done(((f32[64,4,512]{2,1,0:T(4,128)}), f32[64,4,512]{2,1,0:T(4,128)S(1)}, u32[]{:S(2)}, u32[]{:S(2)}) %all-to-all-start.1) | async-done | bytes 524320 | tf_op jit(solution)/shard_map/all_to_all | solution.py:97
  64.1 2.9 %multiply_convert_fusion = (bf16[512,1280]{1,0:T(8,128)(2,1)S(1)}, bf16[512,1280]{1,0:T(8,128)(2,1)S(1)}) fusion(f32[512,1280]{1,0:T(8,128)} %get-tuple-element.24, bf16[8,64,1280]{2,0,1:T(8,128)(2,1)} %copy-done.2, f32[512]{0:T(512)S(1)} %get-tuple-element.10, f32[512]{0:T(512)S(1)} %get-tuple-element.23), kind=kLoop, calls=%fused_computation.4 | loop fusion | flops 4587520 | bytes 6557696 | tf_op jit(solution)/shard_map/convert_element_type | solution.py:93
  66.9 4.0 %copy-done = bf16[4096,1280]{1,0:T(8,128)(2,1)S(1)} copy-done((bf16[4096,1280]{1,0:T(8,128)(2,1)S(1)}, bf16[4096,1280]{1,0:T(8,128)(2,1)}, u32[]{:S(2)}) %copy-start) | copy-done | bytes 10485784
  70.9 4.4 %shard_map.61 = bf16[512,2048]{1,0:T(8,128)(2,1)} custom-call(s32[1]{0:T(128)S(6)} %sub.97.which_ref, bf16[512,1280]{1,0:T(8,128)(2,1)S(1)} %get-tuple-element.11.left_ref, bf16[4096,1280]{1,0:T(8,128)(2,1)S(1)} %copy-done), custom_call_target="tpu_custom_call" | custom-call | flops 2684354560 | bytes 8650752 | tf_op jit(solution)/shard_map/pallas_call | solution.py:30
  75.3 4.4 %shard_map.62 = bf16[512,2048]{1,0:T(8,128)(2,1)} custom-call(s32[1]{0:T(128)S(6)} %sub.97.which_ref, bf16[512,1280]{1,0:T(8,128)(2,1)S(1)} %get-tuple-element.12.left_ref, bf16[4096,1280]{1,0:T(8,128)(2,1)S(1)} %copy-done), custom_call_target="tpu_custom_call" | custom-call | flops 2684354560 | bytes 8650752 | tf_op jit(solution)/shard_map/pallas_call | solution.py:30
  80.3 4.0 %copy-done.1 = bf16[4096,1280]{1,0:T(8,128)(2,1)S(1)} copy-done((bf16[4096,1280]{1,0:T(8,128)(2,1)S(1)}, bf16[4096,1280]{1,0:T(8,128)(2,1)}, u32[]{:S(2)}) %copy-start.1) | copy-done | bytes 10485784
  84.3 3.6 %shard_map.60 = bf16[512,2048]{1,0:T(8,128)(2,1)S(1)} custom-call(s32[1]{0:T(128)} %bitcast.11.which_ref, bf16[512,1280]{1,0:T(8,128)(2,1)S(1)} %get-tuple-element.12.left_ref, bf16[4096,1280]{1,0:T(8,128)(2,1)S(1)} %copy-done.1), custom_call_target="tpu_custom_call" | custom-call | flops 2684354560 | bytes 8650752 | tf_op jit(solution)/shard_map/pallas_call | solution.py:30
  87.9 3.8 %shard_map.59 = f32[512,2048]{1,0:T(8,128)S(1)} custom-call(s32[1]{0:T(128)} %bitcast.11.which_ref, bf16[512,1280]{1,0:T(8,128)(2,1)S(1)} %get-tuple-element.11.left_ref, bf16[4096,1280]{1,0:T(8,128)(2,1)S(1)} %copy-done.1), custom_call_target="tpu_custom_call" | custom-call | flops 2684354560 | bytes 8650752 | tf_op jit(solution)/shard_map/pallas_call | solution.py:30
  91.8 4.2 %add_convert_fusion = bf16[512,2048]{1,0:T(8,128)(2,1)} fusion(bf16[512,2048]{1,0:T(8,128)(2,1)} %collective-permute-done.2, bf16[512,2048]{1,0:T(8,128)(2,1)} %collective-permute-done.1, f32[512,2048]{1,0:T(8,128)S(1)} %shard_map.59, bf16[512,2048]{1,0:T(8,128)(2,1)S(1)} %shard_map.60, f32[512]{0:T(512)S(1)} %get-tuple-element.22, ...), kind=kLoop, calls=%fused_computation.2 | loop fusion | flops 11534336 | bytes 12591104 | tf_op jit(solution)/shard_map/convert_element_type | solution.py:118
  95.9 4.0 %all-to-all-start.2 = ((bf16[32,16,2048]{2,1,0:T(8,128)(2,1)}), bf16[32,16,2048]{2,1,0:T(8,128)(2,1)S(1)}, u32[]{:S(2)}, u32[]{:S(2)}) async-start(bf16[32,16,2048]{2,1,0:T(8,128)(2,1)} %bitcast.52), calls=%async_computation.2 | async-start | bytes 4194304 | tf_op jit(solution)/shard_map/all_to_all | solution.py:119
  100.1 0.7 gather_fusion
  100.7 0.7 slice_reduce_fusion
  102.2 26.6 %all-to-all-done.2 = bf16[32,16,2048]{2,1,0:T(8,128)(2,1)S(1)} async-done(((bf16[32,16,2048]{2,1,0:T(8,128)(2,1)}), bf16[32,16,2048]{2,1,0:T(8,128)(2,1)S(1)}, u32[]{:S(2)}, u32[]{:S(2)}) %all-to-all-start.2) | async-done | bytes 2097184 | tf_op jit(solution)/shard_map/all_to_all | solution.py:119
  129.2 1.7 %collective-permute-start.3 = (bf16[8,2048]{1,0:T(8,128)(2,1)S(1)}, bf16[8,2048]{1,0:T(8,128)(2,1)S(1)}, u32[]{:S(2)}, u32[]{:S(2)}) collective-permute-start(bf16[8,2048]{1,0:T(8,128)(2,1)S(1)} %get-tuple-element.20), channel_id=1, source_target_pairs={{0,1},{1,0},{2,3},{3,2},{4,5},{5,4},{6,7},{7,6},{8,9},{9,8},{10,11... | collective-permute-start | bytes 98312 | tf_op jit(solution)/shard_map/ppermute | solution.py:66
  131.8 0.6 maximum_select_fusion
  (31 shorter events, 2.5 us)
Async XLA Ops:
  0.6 10.4 %copy-start.3 = (s32[2]{0:T(128)S(1)}, s32[2]{0:T(128)}, u32[]{:S(2)}) copy-start(s32[2]{0:T(128)} %param.7) | copy-start | bytes 28
  0.6 31.5 %all-to-all-start = ((bf16[8,64,1280]{2,0,1:T(8,128)(2,1)}), bf16[8,64,1280]{2,0,1:T(8,128)(2,1)S(1)}, u32[]{:S(2)}, u32[]{:S(2)}) async-start(bf16[8,64,1280]{2,0,1:T(8,128)(2,1)} %bitcast.53), calls=%async_computation | async-start | bytes 2621440 | tf_op jit(solution)/shard_map/all_to_all | solution.py:80
  12.3 12.9 %collective-permute-start = (f32[1,1]{1,0:T(1,128)}, f32[1,1]{1,0:T(1,128)}, u32[]{:S(2)}, u32[]{:S(2)}) collective-permute-start(f32[1,1]{1,0:T(1,128)} %bitcast.7), channel_id=1, source_target_pairs={{0,0},{1,1},{2,2},{3,3},{4,4},{5,5},{6,6},{7,7},{8,8},{9,9},{10,10... | collective-permute-start | bytes 20 | tf_op jit(solution)/shard_map/ppermute | solution.py:70
  32.1 4.1 %copy-start.2 = (bf16[8,64,1280]{2,0,1:T(8,128)(2,1)}, bf16[8,64,1280]{2,0,1:T(8,128)(2,1)S(1)}, u32[]{:S(2)}) copy-start(bf16[8,64,1280]{2,0,1:T(8,128)(2,1)S(1)} %all-to-all-done) | copy-start | bytes 3932164
  36.2 27.4 %all-to-all-start.1 = ((f32[64,4,512]{2,1,0:T(4,128)}), f32[64,4,512]{2,1,0:T(4,128)S(1)}, u32[]{:S(2)}, u32[]{:S(2)}) async-start(f32[64,4,512]{2,1,0:T(4,128)} %broadcast_in_dim.5), calls=%async_computation.1 | async-start | bytes 1048576 | tf_op jit(solution)/shard_map/all_to_all | solution.py:97
  66.9 4.0 %copy-start = (bf16[4096,1280]{1,0:T(8,128)(2,1)S(1)}, bf16[4096,1280]{1,0:T(8,128)(2,1)}, u32[]{:S(2)}) copy-start(bf16[4096,1280]{1,0:T(8,128)(2,1)} %weight_ref.7) | copy-start | bytes 31457284
  79.8 12.0 %collective-permute-start.2 = (bf16[512,2048]{1,0:T(8,128)(2,1)}, bf16[512,2048]{1,0:T(8,128)(2,1)}, u32[]{:S(2)}, u32[]{:S(2)}) collective-permute-start(bf16[512,2048]{1,0:T(8,128)(2,1)} %shard_map.62), channel_id=1, source_target_pairs={{0,1},{1,0},{2,3},{3,2},{4,5},{5,4},{6,7},{7,6},{8,9},{9,8},{10,11... | collective-permute-start | bytes 6291464 | tf_op jit(solution)/shard_map/ppermute | solution.py:66
  80.2 11.5 %collective-permute-start.1 = (bf16[512,2048]{1,0:T(8,128)(2,1)}, bf16[512,2048]{1,0:T(8,128)(2,1)}, u32[]{:S(2)}, u32[]{:S(2)}) collective-permute-start(bf16[512,2048]{1,0:T(8,128)(2,1)} %shard_map.61), channel_id=1, source_target_pairs={{0,1},{1,0},{2,3},{3,2},{4,5},{5,4},{6,7},{7,6},{8,9},{9,8},{10,11... | collective-permute-start | bytes 6291464 | tf_op jit(solution)/shard_map/ppermute | solution.py:66
  80.3 4.0 %copy-start.1 = (bf16[4096,1280]{1,0:T(8,128)(2,1)S(1)}, bf16[4096,1280]{1,0:T(8,128)(2,1)}, u32[]{:S(2)}) copy-start(bf16[4096,1280]{1,0:T(8,128)(2,1)} %weight_ref.7) | copy-start | bytes 31457284
  95.9 32.9 %all-to-all-start.2 = ((bf16[32,16,2048]{2,1,0:T(8,128)(2,1)}), bf16[32,16,2048]{2,1,0:T(8,128)(2,1)S(1)}, u32[]{:S(2)}, u32[]{:S(2)}) async-start(bf16[32,16,2048]{2,1,0:T(8,128)(2,1)} %bitcast.52), calls=%async_computation.2 | async-start | bytes 4194304 | tf_op jit(solution)/shard_map/all_to_all | solution.py:119
  129.2 2.6 %collective-permute-start.3 = (bf16[8,2048]{1,0:T(8,128)(2,1)S(1)}, bf16[8,2048]{1,0:T(8,128)(2,1)S(1)}, u32[]{:S(2)}, u32[]{:S(2)}) collective-permute-start(bf16[8,2048]{1,0:T(8,128)(2,1)S(1)} %get-tuple-element.20), channel_id=1, source_target_pairs={{0,1},{1,0},{2,3},{3,2},{4,5},{5,4},{6,7},{7,6},{8,9},{9,8},{10,11... | collective-permute-start | bytes 98312 | tf_op jit(solution)/shard_map/ppermute | solution.py:66

commit v3 on v0

v3 whole, which is shorter than its diff:
```python
import jax
import jax.numpy as jnp
from jax import lax
from jax.experimental import pallas as pl
from jax.experimental.pallas import tpu as pltpu
from jax.sharding import Mesh, PartitionSpec as P

VOCAB = ("y", "x", "z", "core")
ALL = ("seq",) + VOCAB
F32 = jnp.float32
BF16 = jnp.bfloat16
MIB = 2**20
LANES = 128
ACROSS = (((1,), (1,)), ((), ()))


def place_of(memory):
    return pl.BlockSpec(memory_space=memory)


VMEM = place_of(pltpu.VMEM)
HBM = place_of(pltpu.HBM)
SMEM = place_of(pltpu.SMEM)


def shape(*sizes, dtype=F32):
    return jax.ShapeDtypeStruct(sizes, dtype)


def run(kernel, operands, specs, outs, out_specs, scratch=(), limit=62, flops=0):
    return pl.pallas_call(
        kernel,
        out_shape=outs,
        in_specs=specs,
        out_specs=out_specs,
        scratch_shapes=list(scratch),
        compiler_params=pltpu.CompilerParams(vmem_limit_bytes=limit * MIB),
        cost_estimate=pl.CostEstimate(flops=flops, bytes_accessed=0, transcendentals=0),
    )(*operands)


def moves(pairs, sems):
    copies = [pltpu.make_async_copy(a, b, sems.at[k]) for k, (a, b) in enumerate(pairs)]
    for copy in copies:
        copy.start()
    return copies


def packed(columns, rows):
    lane = lax.broadcasted_iota(jnp.int32, (rows, LANES), 1)
    out = jnp.zeros((rows, LANES), F32)
    for k, column in enumerate(columns):
        out = jnp.where(lane == k, column, out)
    return out


def pair_of(stat, other):
    high = jnp.maximum(stat[0:1], other[0:1])
    total = high + jnp.log(jnp.exp(stat[0:1] - high) + jnp.exp(other[0:1] - high))
    share, rest = jnp.exp(stat[0:1] - total), jnp.exp(other[0:1] - total)
    return total, share * stat[1:2] + rest * other[1:2], share, rest


def turned(lines):
    rows = lines[0].shape[1]
    return jnp.concatenate(list(lines) + [jnp.zeros((LANES - len(lines), rows), F32)], axis=0).T


def first_products(where, hidden, weight, lengths):
    rows, depth = hidden.shape
    width = weight.shape[1]
    half = depth // 2
    cuts = 4
    step = depth // cuts

    def kernel(where_ref, lengths_ref, hidden_ref, weight_ref, score_ref, sent_ref, kept_ref, count_ref, left, held, score, probs, sent, kept, sems, out_sems):
        pairs = []
        for k in range(cuts):
            at = pl.ds(k * step, step)
            pairs += [(hidden_ref.at[:, at], left.at[:, at]), (weight_ref.at[at, :], held.at[at, :])]
        copies = moves(pairs, sems)
        total = lengths_ref[0]
        for k in range(1, lengths.shape[0]):
            total = total + lengths_ref[k]
        count_ref[...] = jnp.full(count_ref.shape, total.astype(F32))
        body = pl.ds(0, width)
        for k in range(cuts):
            copies[2 * k].wait()
            copies[2 * k + 1].wait()
            at = pl.ds(k * step, step)
            product = jnp.dot(left[:, at], held[at, :], preferred_element_type=F32)
            if k == 0:
                score[:, body] = product
            else:
                score[:, body] += product
        logits = score[:, body]
        top = jnp.max(logits, axis=1, keepdims=True)
        lse = top + jnp.log(jnp.sum(jnp.exp(logits - top), axis=1, keepdims=True))
        logits = logits - lse
        score[:, body] = logits
        score[:, pl.ds(width, LANES)] = packed((lse,), rows)
        probs[...] = jnp.exp(logits).astype(BF16)
        outs = [(score, score_ref), (sent, sent_ref), (kept, kept_ref)]
        copies = [pltpu.make_async_copy(*pair, out_sems.at[k]) for k, pair in enumerate(outs)]
        copies[0].start()
        core = where_ref[0]
        for k, which in ((1, 1 - core), (2, core)):
            at = pl.ds(pl.multiple_of(which * half, half), half)
            outs[k][0][...] = lax.dot_general(
                probs[...], held[at, :], ACROSS, preferred_element_type=F32
            ).astype(BF16)
            copies[k].start()
        for copy in copies:
            copy.wait()

    return run(
        kernel,
        (where, lengths, hidden, weight),
        [SMEM, SMEM, HBM, HBM],
        [shape(rows, width + LANES)] + [shape(rows, half, dtype=BF16)] * 2 + [shape(8, LANES)],
        [HBM] * 3 + [VMEM],
        [
            pltpu.VMEM((rows, depth), BF16),
            pltpu.VMEM((depth, width), BF16),
            pltpu.VMEM((rows, width + LANES), F32),
            pltpu.VMEM((rows, width), BF16),
            pltpu.VMEM((rows, half), BF16),
            pltpu.VMEM((rows, half), BF16),
            pltpu.SemaphoreType.DMA((2 * cuts,)),
            pltpu.SemaphoreType.DMA((3,)),
        ],
        flops=200 * 10**9,
    )


def middle(score, teacher, devices):
    rows, width = teacher.shape

    def kernel(score_ref, teacher_ref, grad_ref, stats_ref, block_ref, held, target, grad, lines, sems):
        copies = moves([(score_ref, held), (teacher_ref, target)], sems)
        for copy in copies:
            copy.wait()
        score = held[:, pl.ds(0, width)]
        probs = jnp.exp(score)
        advantage = score - target[...].astype(F32)
        mean = jnp.sum(probs * advantage, axis=1, keepdims=True)
        tail = held[:, pl.ds(width, LANES)]
        lse = tail[:, 0:1]
        block = packed((lse, mean + lse), rows).T[:8]
        block_ref[...] = block
        for k in range(devices):
            lines[k] = block[:2]
        stats_copy = pltpu.make_async_copy(lines, stats_ref, sems.at[2])
        stats_copy.start()
        grad[...] = (probs * (advantage - mean)).astype(BF16)
        grad_copy = pltpu.make_async_copy(grad, grad_ref, sems.at[3])
        grad_copy.start()
        stats_copy.wait()
        grad_copy.wait()

    return run(
        kernel,
        (score, teacher),
        [HBM, HBM],
        [
            shape(rows, width, dtype=BF16),
            shape(devices, 2, rows),
            shape(8, rows),
        ],
        [HBM, HBM, VMEM],
        [
            pltpu.VMEM((rows, width + LANES), F32),
            pltpu.VMEM((rows, width), BF16),
            pltpu.VMEM((rows, width), BF16),
            pltpu.VMEM((devices, 2, rows), F32),
            pltpu.SemaphoreType.DMA((4,)),
        ],
        limit=62,
        flops=50 * 10**9,
    )


def pair_products(where, blocks, lefts, weight, weight_far):
    rows, width = lefts[0].shape
    half = weight.shape[0] // 2
    cuts = 4
    step = half // cuts

    def kernel(where_ref, block_ref, block_far_ref, grad_ref, grad_far_ref, weight_ref, far_ref, slope_ref, left, held, slope, factors, sems, out_sems):
        start = pl.multiple_of(where_ref[0] * half, half)
        pairs = []
        for k in range(cuts):
            at = pl.ds(k * step, step)
            here = pl.ds(start + k * step, step)
            for j, (side, ref) in enumerate(((grad_ref, weight_ref), (grad_far_ref, far_ref))):
                if k == 0:
                    pairs.append((side, left.at[j]))
                pairs.append((ref.at[here, :], held.at[j, at, :]))
        copies = moves(pairs, sems)
        stat, other = block_ref[...], block_far_ref[...]
        _, _, share, rest = pair_of(stat, other)
        factors[...] = turned((share, rest))
        outs = []
        for k in range(cuts):
            at = pl.ds(k * step, step)
            total = None
            for j in range(2):
                for copy in copies[2 * j : 2 * j + 2] if k == 0 else copies[2 * k + 2 + j : 2 * k + 3 + j]:
                    copy.wait()
                product = factors[:, j : j + 1] * lax.dot_general(
                    left[j], held[j, at, :], ACROSS, preferred_element_type=F32
                )
                total = product if total is None else total + product
            slope[:, at] = total.astype(BF16)
            outs.append(pltpu.make_async_copy(slope.at[:, at], slope_ref.at[:, at], out_sems.at[k]))
            outs[k].start()
        for copy in outs:
            copy.wait()

    return run(
        kernel,
        (where, *blocks, *lefts, weight, weight_far),
        [SMEM, VMEM, VMEM] + [HBM] * 4,
        [shape(rows, half, dtype=BF16)],
        [HBM],
        [
            pltpu.VMEM((2, rows, width), BF16),
            pltpu.VMEM((2, half, width), BF16),
            pltpu.VMEM((rows, half), BF16),
            pltpu.VMEM((rows, LANES), F32),
            pltpu.SemaphoreType.DMA((2 + 2 * cuts,)),
            pltpu.SemaphoreType.DMA((cuts,)),
        ],
        limit=62,
        flops=200 * 10**9,
    )[0]


def merge(where, lengths, stats, products, counts, planes):
    rows, half = products[0].shape
    slot_count = rows // lengths.shape[0]
    cuts = 4
    step = half // cuts

    def kernel(where_ref, lengths_ref, stats_ref, slope_ref, base_ref, far_ref, count_ref, heard_ref, out_ref, kl_ref, both_ref, held, out, factors, sems, out_sems):
        copies = moves(
            [
                (ref.at[:, pl.ds(k * step, step)], held.at[j, :, pl.ds(k * step, step)])
                for k in range(cuts)
                for j, ref in enumerate((slope_ref, base_ref, far_ref))
            ],
            sems,
        )
        sums = stats_ref[:, 0, :]
        levels = stats_ref[:, 1, :]
        both_ref[...] = count_ref[...] + heard_ref[...]
        high = jnp.max(sums, axis=0, keepdims=True)
        share = jnp.exp(sums - high)
        whole = jnp.sum(share, axis=0, keepdims=True)
        lse = high + jnp.log(whole)
        level = jnp.sum(share * levels, axis=0, keepdims=True) / whole
        token = lax.broadcasted_iota(jnp.int32, (1, rows), 1)
        live = jnp.zeros((1, rows), F32)
        for k in range(rows // slot_count):
            inside = (token >= k * slot_count) & (token < k * slot_count + lengths_ref[k])
            live = jnp.where(inside, 1.0, live)
        start = where_ref[1] * kl_ref.shape[0]
        turn = lax.rem(rows - start, rows)
        kl = jnp.broadcast_to(live * (level - lse), (8, rows))
        kl_ref[...] = pltpu.roll(kl, turn, 1)[0, : kl_ref.shape[0]]
        own, other = (stats_ref[where_ref[k]] for k in (1, 2))
        total, _, near, far = pair_of(own, other)
        factor = live * jnp.exp(total - lse)
        factors[...] = turned(
            (factor, factor * near * (own[1:2] - level), factor * far * (other[1:2] - level))
        )
        outs = []
        for k in range(cuts):
            at = pl.ds(k * step, step)
            value = None
            for j in range(3):
                copies[3 * k + j].wait()
                term = factors[:, j : j + 1] * held[j, :, at].astype(F32)
                value = term if value is None else value + term
            group = rows // stats.shape[0] * 2
            value = value.reshape(rows // (group * planes), planes, group, step)
            for z in range(planes):
                each = rows // planes
                out[pl.ds(z * each, each), at] = value[:, z].reshape(each, step).astype(BF16)
            outs.append(pltpu.make_async_copy(out.at[:, at], out_ref.at[:, at], out_sems.at[k]))
            outs[k].start()
        for copy in outs:
            copy.wait()

    return run(
        kernel,
        (where, lengths, stats, *products, *counts),
        [SMEM, SMEM, VMEM] + [HBM] * 3 + [VMEM] * 2,
        [shape(rows, half, dtype=BF16), shape(rows // stats.shape[0]), shape(8, LANES)],
        [HBM, VMEM, VMEM],
        [
            pltpu.VMEM((3, rows, half), BF16),
            pltpu.VMEM((rows, half), BF16),
            pltpu.VMEM((rows, LANES), F32),
            pltpu.SemaphoreType.DMA((3 * cuts,)),
            pltpu.SemaphoreType.DMA((cuts,)),
        ],
    )


def shares(where, counts, spread, own_rows, scale):
    half = spread.shape[2]

    def kernel(where_ref, spread_ref, *refs):
        keep_ref, give_ref = refs[len(counts) :]
        count = sum(ref[0:1, 0:1] for ref in refs[: len(counts)])
        total = jnp.sum(spread_ref[...].astype(F32), axis=0) * (scale / count)
        first, second = total[:own_rows], total[own_rows:]
        own = where_ref[0] == 0
        keep_ref[...] = jnp.where(own, first, second)
        give_ref[...] = jnp.where(own, second, first)

    return run(
        kernel,
        (where, spread, *counts),
        [SMEM, VMEM] + [VMEM] * len(counts),
        [shape(own_rows, half)] * 2,
        [VMEM] * 2,
        limit=16,
    )


def joined(where, keep, get):
    own_rows, half = keep.shape

    def kernel(where_ref, keep_ref, get_ref, out_ref):
        own = where_ref[0] == 0
        keep, get = keep_ref[...], get_ref[...]
        out_ref[:, :half] = jnp.where(own, keep, get).astype(BF16)
        out_ref[:, half:] = jnp.where(own, get, keep).astype(BF16)

    return run(
        kernel,
        (where, keep, get),
        [SMEM, VMEM, VMEM],
        [shape(own_rows, 2 * half, dtype=BF16)],
        [VMEM],
        limit=16,
    )[0]


def body(student_hidden, head_weight, teacher_logprob, lengths):
    rows, depth = student_hidden.shape
    devices = lax.axis_size(VOCAB)
    own_rows = rows // devices
    seq_devices = lax.axis_size("seq")
    core = lax.axis_index("core").astype(jnp.int32)
    place = lax.axis_index(VOCAB).astype(jnp.int32)
    where = jnp.stack([core, place, place + 1 - 2 * core])

    def swap(value):
        return lax.ppermute(value, "core", [(0, 1), (1, 0)])

    def across(value, bit):
        return lax.ppermute(value, "seq", [(s, s ^ bit) for s in range(seq_devices)])

    def whole(value, axes):
        return lax.all_to_all(value, axes, split_axis=0, concat_axis=0, tiled=True)

    teacher = lax.all_to_all(teacher_logprob, VOCAB, split_axis=1, concat_axis=0, tiled=True)
    weight_far = swap(head_weight)
    score, base_sent, base, count = first_products(where, student_hidden, head_weight, lengths)
    base_far = swap(base_sent)
    counts = (count, across(count, 1))

    grad, stats, block = middle(score, teacher, devices)
    grad_far = swap(grad)
    block_far = swap(block)
    stats = whole(stats, VOCAB)
    slope = pair_products(where, (block, block_far), (grad, grad_far), head_weight, weight_far)

    chip_sum, token_kl, count = merge(
        where, lengths, stats, (slope, base, base_far), counts, lax.axis_size("z")
    )
    spread = whole(chip_sum.reshape(devices // 2, 2 * own_rows, depth // 2), ("z", "y", "x"))
    counts = [count] + [across(count, bit) for bit in range(2, seq_devices, 2)]
    keep, give = shares(where, counts, spread, own_rows, float(rows * seq_devices))
    hidden_grad = joined(where, keep, swap(give))
    return hidden_grad, token_kl


def solution(mesh, sizes=(4, 4, 4, 2, 2)):
    return jax.shard_map(
        body,
        mesh=Mesh(mesh.devices.reshape(sizes), ALL),
        in_specs=(P("seq", None), P(None, VOCAB), P(ALL, None), P("seq")),
        out_specs=(P(ALL, None), P(ALL)),
        check_vma=False,
    )
```

time: 789 us -> 109 us (0.14)
  blocking collectives: 439 us -> 0 us
  waiting for transfers between devices: 293 us -> 24.3 us
  Pallas kernels: 0 us -> 42.8 us
  starting transfers between devices: 10.6 us -> 38.5 us
  matrix products: 21.9 us -> 0 us
  between operations: 15.4 us -> 0.79 us
    psum x3 -> x0, blocking collectives: 300 us -> none  [the longest x1 140 us: body(): total = lax.psum(jnp.sum(jnp.exp(logits - top[:, None]), axis=1), 'vocab')]
    reduce_scatter x1 -> x0, waiting for transfers between devices: 293 us -> none  [body(): lax.psum_scatter(lax.dot_general(grad, head_weight, (((1,), (1,)), ((), (...]
    pmax x1 -> x0, blocking collectives: 139 us -> none  [body(): top = lax.pmax(jnp.max(logits, axis=1), 'vocab')]
    pallas_call x0 -> x6, Pallas kernels: none -> 42.8 us  [run(): pl.pallas_call(kernel, out_shape=outs, in_specs=specs, out_specs=out_spec...]
    ppermute x0 -> x7, waiting for transfers between devices: none -> 23.9 us  [the longest x2 23 us: across(): lax.ppermute(value, 'seq', [(s, s ^ bit) for s in range(seq_devices)])]
    dot_general x2 -> x0, matrix products: 21.9 us -> none  [the longest x1 11.4 us: body(): lax.dot_general(grad, head_weight, (((1,), (1,)), ((), ())), preferred_el...]
    all_to_all x1 -> x3, starting transfers between devices: 10.5 us -> 26.9 us  [the longest x2 16.3 us: whole(): return lax.all_to_all(value, axes, split_axis=0, concat_axis=0, tiled=True)]
    ppermute x0 -> x7, starting transfers between devices: none -> 11.6 us  [the longest x2 7.31 us: across(): lax.ppermute(value, 'seq', [(s, s ^ bit) for s in range(seq_devices)])]
  transfers between devices with their start and end apart: 2 -> 10, of which waited for: 1 -> 3; matrix products, arithmetic and copies ran while one was open for 2% -> 1% of each run, Pallas kernels for 0% -> 32%
where the time goes in v3:
time: 109 us; the launch traced here: 108 us
  Pallas kernels  42.8 us (39%)
  starting transfers between devices  38.5 us (35%)
  waiting for transfers between devices  24.3 us (22%)
  local copies, waits for them, and re-layouts  1.1 us (1%)
    pallas_call x6, Pallas kernels, run(): pl.pallas_call(kernel, out_shape=outs, in_specs=specs, out_specs=out_spec...  42.8 us
    ppermute x2, waiting for transfers between devices, across(): lax.ppermute(value, 'seq', [(s, s ^ bit) for s in range(seq_devices)])  23 us
    all_to_all x2, starting transfers between devices, whole(): return lax.all_to_all(value, axes, split_axis=0, concat_axis=0, tiled=True)  16.3 us
    all_to_all x1, starting transfers between devices, body(): lax.all_to_all(teacher_logprob, VOCAB, split_axis=1, concat_axis=0, tiled...  10.5 us
    ppermute x2, starting transfers between devices, across(): lax.ppermute(value, 'seq', [(s, s ^ bit) for s in range(seq_devices)])  7.31 us
    ppermute x5, starting transfers between devices, swap(): return lax.ppermute(value, 'core', [(0, 1), (1, 0)])  4.33 us
  transfers between devices with their start and end apart: 10, of which 3 were waited for; matrix products, arithmetic and copies ran while one was open for 1% of the time, Pallas kernels for 32%

profile of v3, /device:TPU:1, one launch (start us, length us, event | category | flops | bytes accessed | tf_op | source)
XLA Modules:
  0.0 108.1 jit_solution(15562442477010522237)
XLA Ops:
  0.6 10.5 %all-to-all-start = ((bf16[8,64,1280]{2,0,1:T(8,128)(2,1)}), bf16[8,64,1280]{2,0,1:T(8,128)(2,1)}, u32[]{:S(2)}, u32[]{:S(2)}) async-start(bf16[8,64,1280]{2,0,1:T(8,128)(2,1)} %bitcast.9), calls=%async_computation | async-start | bytes 2621440 | tf_op jit(solution)/shard_map/all_to_all | solution.py:370
  11.2 0.6 collective-permute-start.2
  11.8 0.6 pad_add_fusion.where_ref
  12.4 19.4 %shard_map.59 = (f32[512,1408]{1,0:T(8,128)}, bf16[512,2048]{1,0:T(8,128)(2,1)}, bf16[512,2048]{1,0:T(8,128)(2,1)}, f32[8,128]{1,0:T(8,128)}) custom-call(s32[3]{0:T(128)} %pad_add_fusion.where_ref, s32[2]{0:T(128)} %lengths_ref.3, bf16[512,4096]{1,0:T(8,128)(2,1)} %hidden_ref.1, bf16[4096,1280]{1,0:T(8,128)(2,1)} %weight_ref.3), custom_call_target="tpu_custom_call" | custom-call | flops 199999995904 | tf_op jit(solution)/shard_map/pallas_call | solution.py:31
  31.8 0.4 all-to-all-done
  32.2 5.0 %shard_map.60 = (bf16[512,1280]{1,0:T(8,128)(2,1)}, f32[64,2,512]{2,1,0:T(2,128)}, f32[8,512]{1,0:T(8,128)}) custom-call(f32[512,1408]{1,0:T(8,128)} %get-tuple-element.14.score_ref, bf16[512,1280]{1,0:T(8,128)(2,1)} %bitcast.5.teacher_ref), custom_call_target="tpu_custom_call" | custom-call | flops 49999998976 | tf_op jit(solution)/shard_map/pallas_call | solution.py:31
  37.2 0.8 collective-permute-start.1
  38.0 0.1 collective-permute-start
  38.1 0.4 collective-permute-start.3
  38.5 3.0 %collective-permute-start.4 = (f32[8,128]{1,0:T(8,128)}, f32[8,128]{1,0:T(8,128)}, u32[]{:S(2)}, u32[]{:S(2)}) collective-permute-start(f32[8,128]{1,0:T(8,128)} %get-tuple-element.20.count_ref), channel_id=1, source_target_pairs={{0,64},{64,0},{128,192},{192,128},{1,65},{65,1},{129,193},{193,129... | collective-permute-start | bytes 12296 | tf_op jit(solution)/shard_map/ppermute | solution.py:365
  41.5 8.3 %all-to-all-start.1 = ((f32[64,2,512]{2,1,0:T(2,128)}), f32[64,2,512]{2,1,0:T(2,128)}, u32[]{:S(2)}, u32[]{:S(2)}) async-start(f32[64,2,512]{2,1,0:T(2,128)} %get-tuple-element.15), calls=%async_computation.1 | async-start | bytes 524288 | tf_op jit(solution)/shard_map/all_to_all | solution.py:368
  49.8 0.0 collective-permute-done.block_far_ref
  49.9 0.6 copy-done.3
  50.4 0.5 copy-done.2
  51.0 10.5 %shard_map.61.slope_ref = bf16[512,2048]{1,0:T(8,128)(2,1)} custom-call(s32[3]{0:T(128)} %pad_add_fusion.where_ref, f32[8,512]{1,0:T(8,128)} %get-tuple-element.16.block_ref, f32[8,512]{1,0:T(8,128)} %copy-done.3, bf16[512,1280]{1,0:T(8,128)(2,1)} %get-tuple-element.17.grad_ref, bf16[512,1280]{1,0:T(8,128)(2,1)} %copy-done.2, bf16[4096,1280]{1,0:T(8,128)(2,1)} %weight_ref.3, ...), custom_call_target="tpu_custom_call" | custom-call | flops 199999995904 | tf_op jit(solution)/shard_map/pallas_call | solution.py:31
  61.5 5.8 %shard_map.62 = (bf16[512,2048]{1,0:T(8,128)(2,1)}, f32[8]{0:T(128)}, f32[8,128]{1,0:T(8,128)}) custom-call(s32[3]{0:T(128)} %pad_add_fusion.where_ref, s32[2]{0:T(128)} %lengths_ref.3, f32[64,2,512]{2,1,0:T(2,128)} %all-to-all-done.1.stats_ref, bf16[512,2048]{1,0:T(8,128)(2,1)} %shard_map.61.slope_ref, bf16[512,2048]{1,0:T(8,128)(2,1)} %get-tuple-element.18.base_ref, ...), custom_call_target="tpu_custom_call" | custom-call | tf_op jit(solution)/shard_map/pallas_call | solution.py:31
  67.3 0.0 copy-start.1
  67.3 8.0 %all-to-all-start.2 = ((bf16[32,16,2048]{2,1,0:T(8,128)(2,1)}), bf16[32,16,2048]{2,1,0:T(8,128)(2,1)S(1)}, u32[]{:S(2)}, u32[]{:S(2)}) async-start(bf16[32,16,2048]{2,1,0:T(8,128)(2,1)} %bitcast.8), calls=%async_computation.2 | async-start | bytes 4194304 | tf_op jit(solution)/shard_map/all_to_all | solution.py:368
  75.4 4.3 %collective-permute-start.5 = (f32[8,128]{1,0:T(8,128)S(1)}, f32[8,128]{1,0:T(8,128)S(1)}, u32[]{:S(2)}, u32[]{:S(2)}) collective-permute-start(f32[8,128]{1,0:T(8,128)S(1)} %copy-done.1), channel_id=1, source_target_pairs={{0,128},{64,192},{128,0},{192,64},{1,129},{65,193},{129,1},{193,65... | collective-permute-start | bytes 12296 | tf_op jit(solution)/shard_map/ppermute | solution.py:365
  79.7 23.0 %collective-permute-done.5.refs_1_ = f32[8,128]{1,0:T(8,128)S(1)} collective-permute-done((f32[8,128]{1,0:T(8,128)S(1)}, f32[8,128]{1,0:T(8,128)S(1)}, u32[]{:S(2)}, u32[]{:S(2)}) %collective-permute-start.5) | collective-permute-done | bytes 4128 | tf_op jit(solution)/shard_map/ppermute | solution.py:365
  102.7 1.0 shard_map.63
  103.7 2.4 %collective-permute-start.6 = (f32[8,2048]{1,0:T(8,128)S(1)}, f32[8,2048]{1,0:T(8,128)S(1)}, u32[]{:S(2)}, u32[]{:S(2)}) collective-permute-start(f32[8,2048]{1,0:T(8,128)S(1)} %get-tuple-element.24), channel_id=1, source_target_pairs={{0,1},{1,0},{2,3},{3,2},{4,5},{5,4},{6,7},{7,6},{8,9},{9,8},{10,11... | collective-permute-start | bytes 196616 | tf_op jit(solution)/shard_map/ppermute | solution.py:362
  106.0 0.9 collective-permute-done.6.get_ref
  106.9 1.2 %shard_map.64 = bf16[8,4096]{1,0:T(8,128)(2,1)} custom-call(s32[3]{0:T(128)S(1)} %copy-done, f32[8,2048]{1,0:T(8,128)S(1)} %get-tuple-element.23.keep_ref, f32[8,2048]{1,0:T(8,128)S(1)} %collective-permute-done.6.get_ref), custom_call_target="tpu_custom_call" | custom-call | tf_op jit(solution)/shard_map/pallas_call | solution.py:31
  (11 shorter events, 0.0 us)
Async XLA Ops:
  0.6 31.6 %all-to-all-start = ((bf16[8,64,1280]{2,0,1:T(8,128)(2,1)}), bf16[8,64,1280]{2,0,1:T(8,128)(2,1)}, u32[]{:S(2)}, u32[]{:S(2)}) async-start(bf16[8,64,1280]{2,0,1:T(8,128)(2,1)} %bitcast.9), calls=%async_computation | async-start | bytes 2621440 | tf_op jit(solution)/shard_map/all_to_all | solution.py:370
  11.2 38.7 %collective-permute-start.2 = (bf16[4096,1280]{1,0:T(8,128)(2,1)}, bf16[4096,1280]{1,0:T(8,128)(2,1)}, u32[]{:S(2)}, u32[]{:S(2)}) collective-permute-start(bf16[4096,1280]{1,0:T(8,128)(2,1)} %weight_ref.3), channel_id=1, source_target_pairs={{0,1},{1,0},{2,3},{3,2},{4,5},{5,4},{6,7},{7,6},{8,9},{9,8},{10,11... | collective-permute-start | bytes 31457288 | tf_op jit(solution)/shard_map/ppermute | solution.py:362
  37.2 12.7 %collective-permute-start.1 = (bf16[512,1280]{1,0:T(8,128)(2,1)}, bf16[512,1280]{1,0:T(8,128)(2,1)S(1)}, u32[]{:S(2)}, u32[]{:S(2)}) collective-permute-start(bf16[512,1280]{1,0:T(8,128)(2,1)} %get-tuple-element.17.grad_ref), channel_id=1, source_target_pairs={{0,1},{1,0},{2,3},{3,2},{4,5},{5,4},{6,7},{7,6},{8,9},{9,8},{10,11... | collective-permute-start | bytes 3932168 | tf_op jit(solution)/shard_map/ppermute | solution.py:362
  38.0 11.8 %collective-permute-start = (f32[8,512]{1,0:T(8,128)}, f32[8,512]{1,0:T(8,128)S(1)}, u32[]{:S(2)}, u32[]{:S(2)}) collective-permute-start(f32[8,512]{1,0:T(8,128)} %get-tuple-element.16.block_ref), channel_id=1, source_target_pairs={{0,1},{1,0},{2,3},{3,2},{4,5},{5,4},{6,7},{7,6},{8,9},{9,8},{10,11... | collective-permute-start | bytes 49160 | tf_op jit(solution)/shard_map/ppermute | solution.py:362
  38.1 23.4 %collective-permute-start.3 = (bf16[512,2048]{1,0:T(8,128)(2,1)}, bf16[512,2048]{1,0:T(8,128)(2,1)}, u32[]{:S(2)}, u32[]{:S(2)}) collective-permute-start(bf16[512,2048]{1,0:T(8,128)(2,1)} %get-tuple-element.19), channel_id=1, source_target_pairs={{0,1},{1,0},{2,3},{3,2},{4,5},{5,4},{6,7},{7,6},{8,9},{9,8},{10,11... | collective-permute-start | bytes 6291464 | tf_op jit(solution)/shard_map/ppermute | solution.py:362
  38.5 23.0 %collective-permute-start.4 = (f32[8,128]{1,0:T(8,128)}, f32[8,128]{1,0:T(8,128)}, u32[]{:S(2)}, u32[]{:S(2)}) collective-permute-start(f32[8,128]{1,0:T(8,128)} %get-tuple-element.20.count_ref), channel_id=1, source_target_pairs={{0,64},{64,0},{128,192},{192,128},{1,65},{65,1},{129,193},{193,129... | collective-permute-start | bytes 12296 | tf_op jit(solution)/shard_map/ppermute | solution.py:365
  41.5 20.0 %all-to-all-start.1 = ((f32[64,2,512]{2,1,0:T(2,128)}), f32[64,2,512]{2,1,0:T(2,128)}, u32[]{:S(2)}, u32[]{:S(2)}) async-start(f32[64,2,512]{2,1,0:T(2,128)} %get-tuple-element.15), calls=%async_computation.1 | async-start | bytes 524288 | tf_op jit(solution)/shard_map/all_to_all | solution.py:368
  49.8 0.6 copy-start.3
  49.9 1.1 %copy-start.2 = (bf16[512,1280]{1,0:T(8,128)(2,1)}, bf16[512,1280]{1,0:T(8,128)(2,1)S(1)}, u32[]{:S(2)}) copy-start(bf16[512,1280]{1,0:T(8,128)(2,1)S(1)} %collective-permute-done.1.grad_far_ref) | copy-start | bytes 3932164
  67.3 8.1 %copy-start.1 = (f32[8,128]{1,0:T(8,128)S(1)}, f32[8,128]{1,0:T(8,128)}, u32[]{:S(2)}) copy-start(f32[8,128]{1,0:T(8,128)} %get-tuple-element.22.refs_0_) | copy-start | bytes 12292
  67.3 35.4 %copy-start = (s32[3]{0:T(128)S(1)}, s32[3]{0:T(128)}, u32[]{:S(2)}) copy-start(s32[3]{0:T(128)} %pad_add_fusion.where_ref) | copy-start | bytes 40
  67.3 35.4 %all-to-all-start.2 = ((bf16[32,16,2048]{2,1,0:T(8,128)(2,1)}), bf16[32,16,2048]{2,1,0:T(8,128)(2,1)S(1)}, u32[]{:S(2)}, u32[]{:S(2)}) async-start(bf16[32,16,2048]{2,1,0:T(8,128)(2,1)} %bitcast.8), calls=%async_computation.2 | async-start | bytes 4194304 | tf_op jit(solution)/shard_map/all_to_all | solution.py:368
  75.4 27.3 %collective-permute-start.5 = (f32[8,128]{1,0:T(8,128)S(1)}, f32[8,128]{1,0:T(8,128)S(1)}, u32[]{:S(2)}, u32[]{:S(2)}) collective-permute-start(f32[8,128]{1,0:T(8,128)S(1)} %copy-done.1), channel_id=1, source_target_pairs={{0,128},{64,192},{128,0},{192,64},{1,129},{65,193},{129,1},{193,65... | collective-permute-start | bytes 12296 | tf_op jit(solution)/shard_map/ppermute | solution.py:365
  103.7 3.3 %collective-permute-start.6 = (f32[8,2048]{1,0:T(8,128)S(1)}, f32[8,2048]{1,0:T(8,128)S(1)}, u32[]{:S(2)}, u32[]{:S(2)}) collective-permute-start(f32[8,2048]{1,0:T(8,128)S(1)} %get-tuple-element.24), channel_id=1, source_target_pairs={{0,1},{1,0},{2,3},{3,2},{4,5},{5,4},{6,7},{7,6},{8,9},{9,8},{10,11... | collective-permute-start | bytes 196616 | tf_op jit(solution)/shard_map/ppermute | solution.py:362

commit v4 on v3

v4 whole, which is shorter than its diff:
```python
import jax
import jax.numpy as jnp
from jax import lax
from jax.experimental import pallas as pl
from jax.experimental.pallas import tpu as pltpu
from jax.sharding import Mesh, PartitionSpec as P

VOCAB = ("y", "x", "z", "core")
ALL = ("seq",) + VOCAB
F32 = jnp.float32
BF16 = jnp.bfloat16
MIB = 2**20
LANES = 128
ACROSS = (((1,), (1,)), ((), ()))


def place_of(memory):
    return pl.BlockSpec(memory_space=memory)


VMEM = place_of(pltpu.VMEM)
HBM = place_of(pltpu.HBM)
SMEM = place_of(pltpu.SMEM)


def shape(*sizes, dtype=F32):
    return jax.ShapeDtypeStruct(sizes, dtype)


def run(kernel, operands, specs, outs, out_specs, scratch=(), limit=62, flops=0):
    return pl.pallas_call(
        kernel,
        out_shape=outs,
        in_specs=specs,
        out_specs=out_specs,
        scratch_shapes=list(scratch),
        compiler_params=pltpu.CompilerParams(vmem_limit_bytes=limit * MIB),
        cost_estimate=pl.CostEstimate(flops=flops, bytes_accessed=0, transcendentals=0),
    )(*operands)


def moves(pairs, sems):
    copies = [pltpu.make_async_copy(a, b, sems.at[k]) for k, (a, b) in enumerate(pairs)]
    for copy in copies:
        copy.start()
    return copies


def packed(columns, rows):
    lane = lax.broadcasted_iota(jnp.int32, (rows, LANES), 1)
    out = jnp.zeros((rows, LANES), F32)
    for k, column in enumerate(columns):
        out = jnp.where(lane == k, column, out)
    return out


def turned(lines):
    rows = lines[0].shape[1]
    return jnp.concatenate(list(lines) + [jnp.zeros((LANES - len(lines), rows), F32)], axis=0).T


def first_products(where, hidden, weight, lengths):
    rows, depth = hidden.shape
    width = weight.shape[1]
    half = depth // 2
    cuts = 4
    step = depth // cuts

    def kernel(where_ref, lengths_ref, hidden_ref, weight_ref, score_ref, probs_ref, base_ref, count_ref, left, held, score, probs, base, sems, out_sems):
        pairs = []
        for k in range(cuts):
            at = pl.ds(k * step, step)
            pairs += [(hidden_ref.at[:, at], left.at[:, at]), (weight_ref.at[at, :], held.at[at, :])]
        copies = moves(pairs, sems)
        total = lengths_ref[0]
        for k in range(1, lengths.shape[0]):
            total = total + lengths_ref[k]
        count_ref[...] = jnp.full(count_ref.shape, total.astype(F32))
        body = pl.ds(0, width)
        for k in range(cuts):
            copies[2 * k].wait()
            copies[2 * k + 1].wait()
            at = pl.ds(k * step, step)
            product = jnp.dot(left[:, at], held[at, :], preferred_element_type=F32)
            if k == 0:
                score[:, body] = product
            else:
                score[:, body] += product
        logits = score[:, body]
        top = jnp.max(logits, axis=1, keepdims=True)
        mass = jnp.exp(logits - top)
        total = jnp.sum(mass, axis=1, keepdims=True)
        probs[...] = (mass * (1.0 / total)).astype(BF16)
        outs = [(probs, probs_ref), (score, score_ref), (base, base_ref)]
        copies = [pltpu.make_async_copy(*pair, out_sems.at[k]) for k, pair in enumerate(outs)]
        copies[0].start()
        lse = top + jnp.log(total)
        score[:, body] = logits - lse
        score[:, pl.ds(width, LANES)] = packed((lse,), rows)
        copies[1].start()
        at = pl.ds(pl.multiple_of(where_ref[0] * half, half), half)
        base[...] = lax.dot_general(
            probs[...], held[at, :], ACROSS, preferred_element_type=F32
        ).astype(BF16)
        copies[2].start()
        for copy in copies:
            copy.wait()

    return run(
        kernel,
        (where, lengths, hidden, weight),
        [SMEM, SMEM, HBM, HBM],
        [
            shape(rows, width + LANES),
            shape(rows, width, dtype=BF16),
            shape(rows, half, dtype=BF16),
            shape(8, LANES),
        ],
        [HBM] * 3 + [VMEM],
        [
            pltpu.VMEM((rows, depth), BF16),
            pltpu.VMEM((depth, width), BF16),
            pltpu.VMEM((rows, width + LANES), F32),
            pltpu.VMEM((rows, width), BF16),
            pltpu.VMEM((rows, half), BF16),
            pltpu.SemaphoreType.DMA((2 * cuts,)),
            pltpu.SemaphoreType.DMA((3,)),
        ],
        flops=200 * 10**9,
    )


def near_product(where, left, weight):
    rows, width = left.shape
    half = weight.shape[0] // 2
    cuts = 4
    step = half // cuts

    def kernel(where_ref, left_ref, weight_ref, out_ref, side, held, out, sems, out_sems):
        start = pl.multiple_of(where_ref[0] * half, half)
        pairs = [(left_ref, side)]
        for k in range(cuts):
            pairs.append((weight_ref.at[pl.ds(start + k * step, step), :], held.at[pl.ds(k * step, step), :]))
        copies = moves(pairs, sems)
        copies[0].wait()
        outs = []
        for k in range(cuts):
            at = pl.ds(k * step, step)
            copies[1 + k].wait()
            out[:, at] = lax.dot_general(
                side[...], held[at, :], ACROSS, preferred_element_type=F32
            ).astype(BF16)
            outs.append(pltpu.make_async_copy(out.at[:, at], out_ref.at[:, at], out_sems.at[k]))
            outs[k].start()
        for copy in outs:
            copy.wait()

    return run(
        kernel,
        (where, left, weight),
        [SMEM, HBM, HBM],
        [shape(rows, half, dtype=BF16)],
        [HBM],
        [
            pltpu.VMEM((rows, width), BF16),
            pltpu.VMEM((half, width), BF16),
            pltpu.VMEM((rows, half), BF16),
            pltpu.SemaphoreType.DMA((1 + cuts,)),
            pltpu.SemaphoreType.DMA((cuts,)),
        ],
        flops=50 * 10**9,
    )[0]


def middle(score, teacher, devices):
    rows, width = teacher.shape

    def kernel(score_ref, teacher_ref, grad_ref, stats_ref, held, target, grad, lines, sems):
        copies = moves([(score_ref, held), (teacher_ref, target)], sems)
        for copy in copies:
            copy.wait()
        score = held[:, pl.ds(0, width)]
        probs = jnp.exp(score)
        advantage = score - target[...].astype(F32)
        mean = jnp.sum(probs * advantage, axis=1, keepdims=True)
        lse = held[:, pl.ds(width, LANES)][:, 0:1]
        block = packed((lse, mean + lse), rows).T[:2]
        for k in range(devices):
            lines[k] = block
        stats_copy = pltpu.make_async_copy(lines, stats_ref, sems.at[2])
        stats_copy.start()
        grad[...] = (probs * (advantage - mean)).astype(BF16)
        grad_copy = pltpu.make_async_copy(grad, grad_ref, sems.at[3])
        grad_copy.start()
        stats_copy.wait()
        grad_copy.wait()

    return run(
        kernel,
        (score, teacher),
        [HBM, HBM],
        [shape(rows, width, dtype=BF16), shape(devices, 2, rows)],
        [HBM, HBM],
        [
            pltpu.VMEM((rows, width + LANES), F32),
            pltpu.VMEM((rows, width), BF16),
            pltpu.VMEM((rows, width), BF16),
            pltpu.VMEM((devices, 2, rows), F32),
            pltpu.SemaphoreType.DMA((4,)),
        ],
        flops=50 * 10**9,
    )


def chip_products(where, lengths, stats, lefts, weight_far, products, counts, planes):
    rows, half = products[0].shape
    width = weight_far.shape[1]
    slot_count = rows // lengths.shape[0]
    cuts = 4
    step = half // cuts

    def kernel(where_ref, lengths_ref, stats_ref, grad_ref, probs_ref, far_ref, near_ref, base_ref, count_ref, out_ref, kl_ref, passed_ref, left, side, held, mine, out, factors, sems, out_sems):
        start = pl.multiple_of(where_ref[0] * half, half)
        pairs = [(grad_ref, left.at[0]), (probs_ref, left.at[1])]
        for k in range(cuts):
            at = pl.ds(k * step, step)
            pairs += [
                (far_ref.at[pl.ds(start + k * step, step), :], held.at[at, :]),
                (near_ref.at[:, at], mine.at[0, :, at]),
                (base_ref.at[:, at], mine.at[1, :, at]),
            ]
        copies = moves(pairs, sems)
        passed_ref[...] = count_ref[...]
        sums = stats_ref[:, 0, :]
        levels = stats_ref[:, 1, :]
        high = jnp.max(sums, axis=0, keepdims=True)
        share = jnp.exp(sums - high)
        whole = jnp.sum(share, axis=0, keepdims=True)
        lse = high + jnp.log(whole)
        level = jnp.sum(share * levels, axis=0, keepdims=True) / whole
        token = lax.broadcasted_iota(jnp.int32, (1, rows), 1)
        live = jnp.zeros((1, rows), F32)
        for k in range(rows // slot_count):
            inside = (token >= k * slot_count) & (token < k * slot_count + lengths_ref[k])
            live = jnp.where(inside, 1.0, live)
        own_rows = kl_ref.shape[0]
        turn = lax.rem(rows - where_ref[1] * own_rows, rows)
        kl = jnp.broadcast_to(live * (level - lse), (8, rows))
        kl_ref[...] = pltpu.roll(kl, turn, 1)[0, :own_rows]
        lines = []
        for k in (1, 2):
            stat = stats_ref[where_ref[k]]
            factor = live * jnp.exp(stat[0:1] - lse)
            lines += [factor, factor * (stat[1:2] - level)]
        factors[...] = turned(lines)
        copies[0].wait()
        copies[1].wait()
        side[...] = (
            factors[:, 2:3] * left[0].astype(F32) + factors[:, 3:4] * left[1].astype(F32)
        ).astype(BF16)
        outs = []
        group = rows // stats.shape[0] * 2
        each = rows // planes
        for k in range(cuts):
            at = pl.ds(k * step, step)
            for j in range(3):
                copies[2 + 3 * k + j].wait()
            value = lax.dot_general(side[...], held[at, :], ACROSS, preferred_element_type=F32)
            for j in range(2):
                value = value + factors[:, j : j + 1] * mine[j, :, at].astype(F32)
            value = value.reshape(rows // (group * planes), planes, group, step)
            for z in range(planes):
                out[pl.ds(z * each, each), at] = value[:, z].reshape(each, step).astype(BF16)
            outs.append(pltpu.make_async_copy(out.at[:, at], out_ref.at[:, at], out_sems.at[k]))
            outs[k].start()
        for copy in outs:
            copy.wait()

    return run(
        kernel,
        (where, lengths, stats, *lefts, weight_far, *products, *counts),
        [SMEM, SMEM, VMEM] + [HBM] * 5 + [VMEM],
        [shape(rows, half, dtype=BF16), shape(rows // stats.shape[0]), shape(8, LANES)],
        [HBM, VMEM, VMEM],
        [
            pltpu.VMEM((2, rows, width), BF16),
            pltpu.VMEM((rows, width), BF16),
            pltpu.VMEM((half, width), BF16),
            pltpu.VMEM((2, rows, half), BF16),
            pltpu.VMEM((rows, half), BF16),
            pltpu.VMEM((rows, LANES), F32),
            pltpu.SemaphoreType.DMA((2 + 3 * cuts,)),
            pltpu.SemaphoreType.DMA((cuts,)),
        ],
    )


def body(student_hidden, head_weight, teacher_logprob, lengths):
    rows, depth = student_hidden.shape
    devices = lax.axis_size(VOCAB)
    own_rows = rows // devices
    seq_devices = lax.axis_size("seq")
    core = lax.axis_index("core").astype(jnp.int32)
    place = lax.axis_index(VOCAB).astype(jnp.int32)
    where = jnp.stack([core, place, place + 1 - 2 * core])

    def swap(value):
        return lax.ppermute(value, "core", [(0, 1), (1, 0)])

    def across(value, step):
        return lax.ppermute(value, "seq", [(s, (s + step) % seq_devices) for s in range(seq_devices)])

    def whole(value, axes):
        return lax.all_to_all(value, axes, split_axis=0, concat_axis=0, tiled=True)

    teacher = lax.all_to_all(teacher_logprob, VOCAB, split_axis=1, concat_axis=0, tiled=True)
    weight_far = swap(head_weight)
    score, probs, base, count = first_products(where, student_hidden, head_weight, lengths)
    probs_far = swap(probs)

    grad, stats = middle(score, teacher, devices)
    grad_far = swap(grad)
    stats = whole(stats, VOCAB)
    near = near_product(where, grad, head_weight)

    chip_sum, token_kl, count = chip_products(
        where,
        lengths,
        stats,
        (grad_far, probs_far),
        weight_far,
        (near, base),
        (count,),
        lax.axis_size("z"),
    )
    spread = whole(chip_sum.reshape(devices // 2, 2 * own_rows, depth // 2), ("z", "y", "x"))
    count = count + sum(across(count, step) for step in range(1, seq_devices))
    summed = jnp.sum(spread.astype(F32), axis=0) * (float(rows * seq_devices) / count[0, 0])
    first, second = summed[:own_rows], summed[own_rows:]
    own = core == 0
    keep = jnp.where(own, first, second).astype(BF16)
    get = swap(jnp.where(own, second, first).astype(BF16))
    hidden_grad = jnp.concatenate([jnp.where(own, keep, get), jnp.where(own, get, keep)], axis=1)
    return hidden_grad, token_kl


def solution(mesh, sizes=(4, 4, 4, 2, 2)):
    return jax.shard_map(
        body,
        mesh=Mesh(mesh.devices.reshape(sizes), ALL),
        in_specs=(P("seq", None), P(None, VOCAB), P(ALL, None), P("seq")),
        out_specs=(P(ALL, None), P(ALL)),
        check_vma=False,
    )
```

time: 109 us -> 102 us (0.936)
  Pallas kernels: 42.8 us -> 36.4 us
  starting transfers between devices: 38.5 us -> 33.5 us
  waiting for transfers between devices: 24.3 us -> 27.6 us
    pallas_call x6 -> x4, Pallas kernels: 42.8 us -> 36.4 us  [run(): pl.pallas_call(kernel, out_shape=outs, in_specs=specs, out_specs=out_spec...]
    all_to_all x2, starting transfers between devices: 16.3 us -> 11.6 us  [whole(): return lax.all_to_all(value, axes, split_axis=0, concat_axis=0, tiled=True)]
    all_to_all x1, waiting for transfers between devices: 0.41 us -> 3.08 us  [body(): lax.all_to_all(teacher_logprob, VOCAB, split_axis=1, concat_axis=0, tiled...]
    all_to_all x2, waiting for transfers between devices: 0.01 us -> 2.46 us  [whole(): return lax.all_to_all(value, axes, split_axis=0, concat_axis=0, tiled=True)]
    ppermute x2 -> x3, waiting for transfers between devices: 23 us -> 21.2 us  [across(): lax.ppermute(value, 'seq', [(s, (s + step) % seq_devices) for s in range(...]
    ppermute x5 -> x4, starting transfers between devices: 4.33 us -> 2.86 us  [swap(): return lax.ppermute(value, 'core', [(0, 1), (1, 0)])]
    ppermute x2 -> x3, starting transfers between devices: 7.31 us -> 8.44 us  [across(): lax.ppermute(value, 'seq', [(s, (s + step) % seq_devices) for s in range(...]
  transfers between devices with their start and end apart: 10 -> 10, of which waited for: 3 -> 4; matrix products, arithmetic and copies ran while one was open for 1% -> 1% of each run, Pallas kernels for 32% -> 27%
where the time goes in v4:
time: 102 us
  Pallas kernels  36.4 us (36%)
  starting transfers between devices  33.5 us (33%)
  waiting for transfers between devices  27.6 us (27%)
  other arithmetic  1.58 us (2%)
  between operations  1.47 us (1%)
  local copies, waits for them, and re-layouts  1.22 us (1%)
    pallas_call x4, Pallas kernels, run(): pl.pallas_call(kernel, out_shape=outs, in_specs=specs, out_specs=out_spec...  36.4 us
    ppermute x3, waiting for transfers between devices, across(): lax.ppermute(value, 'seq', [(s, (s + step) % seq_devices) for s in range(...  21.2 us
    all_to_all x2, starting transfers between devices, whole(): return lax.all_to_all(value, axes, split_axis=0, concat_axis=0, tiled=True)  11.6 us
    all_to_all x1, starting transfers between devices, body(): lax.all_to_all(teacher_logprob, VOCAB, split_axis=1, concat_axis=0, tiled...  10.5 us
    ppermute x3, starting transfers between devices, across(): lax.ppermute(value, 'seq', [(s, (s + step) % seq_devices) for s in range(...  8.44 us
    all_to_all x1, waiting for transfers between devices, body(): lax.all_to_all(teacher_logprob, VOCAB, split_axis=1, concat_axis=0, tiled...  3.08 us
    ppermute x4, starting transfers between devices, swap(): return lax.ppermute(value, 'core', [(0, 1), (1, 0)])  2.86 us
    all_to_all x2, waiting for transfers between devices, whole(): return lax.all_to_all(value, axes, split_axis=0, concat_axis=0, tiled=True)  2.46 us
  transfers between devices with their start and end apart: 10, of which 4 were waited for; matrix products, arithmetic and copies ran while one was open for 1% of the time, Pallas kernels for 27%

profile of v4, /device:TPU:1, one launch (start us, length us, event | category | flops | bytes accessed | tf_op | source)
XLA Modules:
  0.0 101.7 jit_solution(4977919855176169144)
XLA Ops:
  0.6 10.5 %all-to-all-start = ((bf16[8,64,1280]{2,0,1:T(8,128)(2,1)}), bf16[8,64,1280]{2,0,1:T(8,128)(2,1)}, u32[]{:S(2)}, u32[]{:S(2)}) async-start(bf16[8,64,1280]{2,0,1:T(8,128)(2,1)} %bitcast.10), calls=%async_computation | async-start | bytes 2621440 | tf_op jit(solution)/shard_map/all_to_all | solution.py:316
  11.2 0.6 collective-permute-start.2
  11.8 0.6 pad_add_fusion.where_ref
  12.3 16.6 %shard_map.59 = (f32[512,1408]{1,0:T(8,128)}, bf16[512,1280]{1,0:T(8,128)(2,1)}, bf16[512,2048]{1,0:T(8,128)(2,1)}, f32[8,128]{1,0:T(8,128)}) custom-call(s32[3]{0:T(128)} %pad_add_fusion.where_ref, s32[2]{0:T(128)} %lengths_ref.3, bf16[512,4096]{1,0:T(8,128)(2,1)} %hidden_ref.1, bf16[4096,1280]{1,0:T(8,128)(2,1)} %weight_ref.3), custom_call_target="tpu_custom_call" | custom-call | flops 199999995904 | tf_op jit(solution)/shard_map/pallas_call | solution.py:31
  29.0 0.1 collective-permute-start.1
  29.1 3.1 %all-to-all-done = bf16[8,64,1280]{2,0,1:T(8,128)(2,1)} async-done(((bf16[8,64,1280]{2,0,1:T(8,128)(2,1)}), bf16[8,64,1280]{2,0,1:T(8,128)(2,1)}, u32[]{:S(2)}, u32[]{:S(2)}) %all-to-all-start) | async-done | bytes 1310752 | tf_op jit(solution)/shard_map/all_to_all | solution.py:316
  32.2 4.3 %shard_map.60 = (bf16[512,1280]{1,0:T(8,128)(2,1)}, f32[64,2,512]{2,1,0:T(2,128)}) custom-call(f32[512,1408]{1,0:T(8,128)} %get-tuple-element.11.score_ref, bf16[512,1280]{1,0:T(8,128)(2,1)} %bitcast.5.teacher_ref), custom_call_target="tpu_custom_call" | custom-call | flops 49999998976 | tf_op jit(solution)/shard_map/pallas_call | solution.py:31
  36.5 5.7 %all-to-all-start.1 = ((f32[64,2,512]{2,1,0:T(2,128)}), f32[64,2,512]{2,1,0:T(2,128)S(1)}, u32[]{:S(2)}, u32[]{:S(2)}) async-start(f32[64,2,512]{2,1,0:T(2,128)} %get-tuple-element.12), calls=%async_computation.1 | async-start | bytes 524288 | tf_op jit(solution)/shard_map/all_to_all | solution.py:314
  42.3 0.7 collective-permute-start
  43.0 6.8 %shard_map.61.near_ref = bf16[512,2048]{1,0:T(8,128)(2,1)} custom-call(s32[3]{0:T(128)} %pad_add_fusion.where_ref, bf16[512,1280]{1,0:T(8,128)(2,1)} %get-tuple-element.13.left_ref, bf16[4096,1280]{1,0:T(8,128)(2,1)} %weight_ref.3), custom_call_target="tpu_custom_call" | custom-call | flops 49999998976 | tf_op jit(solution)/shard_map/pallas_call | solution.py:31
  49.8 2.5 %all-to-all-done.1.stats_ref = f32[64,2,512]{2,1,0:T(2,128)S(1)} async-done(((f32[64,2,512]{2,1,0:T(2,128)}), f32[64,2,512]{2,1,0:T(2,128)S(1)}, u32[]{:S(2)}, u32[]{:S(2)}) %all-to-all-start.1) | async-done | bytes 262176 | tf_op jit(solution)/shard_map/all_to_all | solution.py:314
  52.3 0.7 copy-done.1
  53.0 8.7 %shard_map.62 = (bf16[512,2048]{1,0:T(8,128)(2,1)}, f32[8]{0:T(128)}, f32[8,128]{1,0:T(8,128)}) custom-call(s32[3]{0:T(128)} %pad_add_fusion.where_ref, s32[2]{0:T(128)} %lengths_ref.3, f32[64,2,512]{2,1,0:T(2,128)} %copy-done.1, bf16[512,1280]{1,0:T(8,128)(2,1)} %collective-permute-done.grad_ref, bf16[512,1280]{1,0:T(8,128)(2,1)} %copy-done, ...), custom_call_target="tpu_custom_call" | custom-call | tf_op jit(solution)/shard_map/pallas_call | solution.py:31
  61.7 5.9 %all-to-all-start.2 = ((bf16[32,16,2048]{2,1,0:T(8,128)(2,1)}), bf16[32,16,2048]{2,1,0:T(8,128)(2,1)S(1)}, u32[]{:S(2)}, u32[]{:S(2)}) async-start(bf16[32,16,2048]{2,1,0:T(8,128)(2,1)} %bitcast.9), calls=%async_computation.2 | async-start | bytes 4194304 | tf_op jit(solution)/shard_map/all_to_all | solution.py:314
  67.6 5.2 %collective-permute-start.5 = (f32[8,128]{1,0:T(8,128)S(1)}, f32[8,128]{1,0:T(8,128)S(1)}, u32[]{:S(2)}, u32[]{:S(2)}) collective-permute-start(f32[8,128]{1,0:T(8,128)S(1)} %copy-done.2), channel_id=1, source_target_pairs={{0,192},{64,0},{128,64},{192,128},{1,193},{65,1},{129,65},{193,129... | collective-permute-start | bytes 12296 | tf_op jit(solution)/shard_map/ppermute | solution.py:311
  72.8 1.2 %collective-permute-start.4 = (f32[8,128]{1,0:T(8,128)S(1)}, f32[8,128]{1,0:T(8,128)S(1)}, u32[]{:S(2)}, u32[]{:S(2)}) collective-permute-start(f32[8,128]{1,0:T(8,128)S(1)} %copy-done.2), channel_id=1, source_target_pairs={{0,128},{64,192},{128,0},{192,64},{1,129},{65,193},{129,1},{193,65... | collective-permute-start | bytes 12296 | tf_op jit(solution)/shard_map/ppermute | solution.py:311
  73.9 2.1 %collective-permute-start.3 = (f32[8,128]{1,0:T(8,128)S(1)}, f32[8,128]{1,0:T(8,128)S(1)}, u32[]{:S(2)}, u32[]{:S(2)}) collective-permute-start(f32[8,128]{1,0:T(8,128)S(1)} %copy-done.2), channel_id=1, source_target_pairs={{0,64},{64,128},{128,192},{192,0},{1,65},{65,129},{129,193},{193,1... | collective-permute-start | bytes 12296 | tf_op jit(solution)/shard_map/ppermute | solution.py:311
  76.0 0.0 collective-permute-done.5
  76.0 21.2 %collective-permute-done.4 = f32[8,128]{1,0:T(8,128)S(1)} collective-permute-done((f32[8,128]{1,0:T(8,128)S(1)}, f32[8,128]{1,0:T(8,128)S(1)}, u32[]{:S(2)}, u32[]{:S(2)}) %collective-permute-start.4) | collective-permute-done | bytes 4128 | tf_op jit(solution)/shard_map/ppermute | solution.py:311
  97.2 0.5 slice.9
  98.4 0.3 convert_reduce_fusion
  98.8 1.4 %collective-permute-start.6 = (bf16[8,2048]{1,0:T(8,128)(2,1)S(1)}, bf16[8,2048]{1,0:T(8,128)(2,1)S(1)}, u32[]{:S(2)}, u32[]{:S(2)}) collective-permute-start(bf16[8,2048]{1,0:T(8,128)(2,1)S(1)} %select_convert_fusion), channel_id=1, source_target_pairs={{0,1},{1,0},{2,3},{3,2},{4,5},{5,4},{6,7},{7,6},{8,9},{9,8},{10,11... | collective-permute-start | bytes 98312 | tf_op jit(solution)/shard_map/ppermute | solution.py:308
  100.2 0.9 collective-permute-done.6
  101.1 0.6 pad_maximum_fusion
  (15 shorter events, 0.1 us)
Async XLA Ops:
  0.6 31.6 %all-to-all-start = ((bf16[8,64,1280]{2,0,1:T(8,128)(2,1)}), bf16[8,64,1280]{2,0,1:T(8,128)(2,1)}, u32[]{:S(2)}, u32[]{:S(2)}) async-start(bf16[8,64,1280]{2,0,1:T(8,128)(2,1)} %bitcast.10), calls=%async_computation | async-start | bytes 2621440 | tf_op jit(solution)/shard_map/all_to_all | solution.py:316
  11.2 41.1 %collective-permute-start.2 = (bf16[4096,1280]{1,0:T(8,128)(2,1)}, bf16[4096,1280]{1,0:T(8,128)(2,1)}, u32[]{:S(2)}, u32[]{:S(2)}) collective-permute-start(bf16[4096,1280]{1,0:T(8,128)(2,1)} %weight_ref.3), channel_id=1, source_target_pairs={{0,1},{1,0},{2,3},{3,2},{4,5},{5,4},{6,7},{7,6},{8,9},{9,8},{10,11... | collective-permute-start | bytes 31457288 | tf_op jit(solution)/shard_map/ppermute | solution.py:308
  29.0 20.8 %collective-permute-start.1 = (bf16[512,1280]{1,0:T(8,128)(2,1)}, bf16[512,1280]{1,0:T(8,128)(2,1)S(1)}, u32[]{:S(2)}, u32[]{:S(2)}) collective-permute-start(bf16[512,1280]{1,0:T(8,128)(2,1)} %get-tuple-element.14), channel_id=1, source_target_pairs={{0,1},{1,0},{2,3},{3,2},{4,5},{5,4},{6,7},{7,6},{8,9},{9,8},{10,11... | collective-permute-start | bytes 3932168 | tf_op jit(solution)/shard_map/ppermute | solution.py:308
  36.5 15.7 %all-to-all-start.1 = ((f32[64,2,512]{2,1,0:T(2,128)}), f32[64,2,512]{2,1,0:T(2,128)S(1)}, u32[]{:S(2)}, u32[]{:S(2)}) async-start(f32[64,2,512]{2,1,0:T(2,128)} %get-tuple-element.12), calls=%async_computation.1 | async-start | bytes 524288 | tf_op jit(solution)/shard_map/all_to_all | solution.py:314
  42.3 10.0 %collective-permute-start = (bf16[512,1280]{1,0:T(8,128)(2,1)}, bf16[512,1280]{1,0:T(8,128)(2,1)}, u32[]{:S(2)}, u32[]{:S(2)}) collective-permute-start(bf16[512,1280]{1,0:T(8,128)(2,1)} %get-tuple-element.13.left_ref), channel_id=1, source_target_pairs={{0,1},{1,0},{2,3},{3,2},{4,5},{5,4},{6,7},{7,6},{8,9},{9,8},{10,11... | collective-permute-start | bytes 3932168 | tf_op jit(solution)/shard_map/ppermute | solution.py:308
  49.8 2.5 %copy-start = (bf16[512,1280]{1,0:T(8,128)(2,1)}, bf16[512,1280]{1,0:T(8,128)(2,1)S(1)}, u32[]{:S(2)}) copy-start(bf16[512,1280]{1,0:T(8,128)(2,1)S(1)} %collective-permute-done.1.probs_ref) | copy-start | bytes 3932164
  52.3 0.7 copy-start.1
  61.6 5.9 %copy-start.2 = (f32[8,128]{1,0:T(8,128)S(1)}, f32[8,128]{1,0:T(8,128)}, u32[]{:S(2)}) copy-start(f32[8,128]{1,0:T(8,128)} %get-tuple-element.18) | copy-start | bytes 12292
  61.7 36.8 %all-to-all-start.2 = ((bf16[32,16,2048]{2,1,0:T(8,128)(2,1)}), bf16[32,16,2048]{2,1,0:T(8,128)(2,1)S(1)}, u32[]{:S(2)}, u32[]{:S(2)}) async-start(bf16[32,16,2048]{2,1,0:T(8,128)(2,1)} %bitcast.9), calls=%async_computation.2 | async-start | bytes 4194304 | tf_op jit(solution)/shard_map/all_to_all | solution.py:314
  67.6 8.4 %collective-permute-start.5 = (f32[8,128]{1,0:T(8,128)S(1)}, f32[8,128]{1,0:T(8,128)S(1)}, u32[]{:S(2)}, u32[]{:S(2)}) collective-permute-start(f32[8,128]{1,0:T(8,128)S(1)} %copy-done.2), channel_id=1, source_target_pairs={{0,192},{64,0},{128,64},{192,128},{1,193},{65,1},{129,65},{193,129... | collective-permute-start | bytes 12296 | tf_op jit(solution)/shard_map/ppermute | solution.py:311
  72.8 24.4 %collective-permute-start.4 = (f32[8,128]{1,0:T(8,128)S(1)}, f32[8,128]{1,0:T(8,128)S(1)}, u32[]{:S(2)}, u32[]{:S(2)}) collective-permute-start(f32[8,128]{1,0:T(8,128)S(1)} %copy-done.2), channel_id=1, source_target_pairs={{0,128},{64,192},{128,0},{192,64},{1,129},{65,193},{129,1},{193,65... | collective-permute-start | bytes 12296 | tf_op jit(solution)/shard_map/ppermute | solution.py:311
  73.9 23.3 %collective-permute-start.3 = (f32[8,128]{1,0:T(8,128)S(1)}, f32[8,128]{1,0:T(8,128)S(1)}, u32[]{:S(2)}, u32[]{:S(2)}) collective-permute-start(f32[8,128]{1,0:T(8,128)S(1)} %copy-done.2), channel_id=1, source_target_pairs={{0,64},{64,128},{128,192},{192,0},{1,65},{65,129},{129,193},{193,1... | collective-permute-start | bytes 12296 | tf_op jit(solution)/shard_map/ppermute | solution.py:311
  98.8 2.3 %collective-permute-start.6 = (bf16[8,2048]{1,0:T(8,128)(2,1)S(1)}, bf16[8,2048]{1,0:T(8,128)(2,1)S(1)}, u32[]{:S(2)}, u32[]{:S(2)}) collective-permute-start(bf16[8,2048]{1,0:T(8,128)(2,1)S(1)} %select_convert_fusion), channel_id=1, source_target_pairs={{0,1},{1,0},{2,3},{3,2},{4,5},{5,4},{6,7},{7,6},{8,9},{9,8},{10,11... | collective-permute-start | bytes 98312 | tf_op jit(solution)/shard_map/ppermute | solution.py:308

commit v5 on v4

--- a/solution.py
+++ b/solution.py
@@ -212,7 +212,8 @@
     )
 
 
-def chip_products(where, lengths, stats, lefts, weight_far, products, counts, planes):
+def chip_products(where, lengths, stats, lefts, weight_far, products, counts, sizes):
+    ny, nx, nz = sizes
     rows, half = products[0].shape
     width = weight_far.shape[1]
     slot_count = rows // lengths.shape[0]
@@ -221,7 +222,7 @@
 
     def kernel(where_ref, lengths_ref, stats_ref, grad_ref, probs_ref, far_ref, near_ref, base_ref, count_ref, out_ref, kl_ref, passed_ref, left, side, held, mine, out, factors, sems, out_sems):
         start = pl.multiple_of(where_ref[0] * half, half)
-        pairs = [(grad_ref, left.at[0]), (probs_ref, left.at[1])]
+        pairs = [(grad_ref, left)]
         for k in range(cuts):
             at = pl.ds(k * step, step)
             pairs += [
@@ -254,23 +255,26 @@
             lines += [factor, factor * (stat[1:2] - level)]
         factors[...] = turned(lines)
         copies[0].wait()
-        copies[1].wait()
         side[...] = (
-            factors[:, 2:3] * left[0].astype(F32) + factors[:, 3:4] * left[1].astype(F32)
+            factors[:, 2:3] * left[...].astype(F32) + factors[:, 3:4] * probs_ref[...].astype(F32)
         ).astype(BF16)
         outs = []
-        group = rows // stats.shape[0] * 2
-        each = rows // planes
         for k in range(cuts):
             at = pl.ds(k * step, step)
             for j in range(3):
-                copies[2 + 3 * k + j].wait()
+                copies[1 + 3 * k + j].wait()
             value = lax.dot_general(side[...], held[at, :], ACROSS, preferred_element_type=F32)
             for j in range(2):
                 value = value + factors[:, j : j + 1] * mine[j, :, at].astype(F32)
-            value = value.reshape(rows // (group * planes), planes, group, step)
-            for z in range(planes):
-                out[pl.ds(z * each, each), at] = value[:, z].reshape(each, step).astype(BF16)
+            value = value.reshape(ny, nx * nz * 2, own_rows, step)
+            each = ny * own_rows
+            for x in range(nx):
+                for z in range(nz):
+                    for c in range(2):
+                        spot = (c * nz + z) * nx + x
+                        out[pl.ds(spot * each, each), at] = (
+                            value[:, (x * nz + z) * 2 + c].reshape(each, step).astype(BF16)
+                        )
             outs.append(pltpu.make_async_copy(out.at[:, at], out_ref.at[:, at], out_sems.at[k]))
             outs[k].start()
         for copy in outs:
@@ -279,19 +283,20 @@
     return run(
         kernel,
         (where, lengths, stats, *lefts, weight_far, *products, *counts),
-        [SMEM, SMEM, VMEM] + [HBM] * 5 + [VMEM],
+        [SMEM, SMEM, VMEM, HBM, VMEM] + [HBM] * 3 + [VMEM],
         [shape(rows, half, dtype=BF16), shape(rows // stats.shape[0]), shape(8, LANES)],
         [HBM, VMEM, VMEM],
         [
-            pltpu.VMEM((2, rows, width), BF16),
+            pltpu.VMEM((rows, width), BF16),
             pltpu.VMEM((rows, width), BF16),
             pltpu.VMEM((half, width), BF16),
             pltpu.VMEM((2, rows, half), BF16),
             pltpu.VMEM((rows, half), BF16),
             pltpu.VMEM((rows, LANES), F32),
-            pltpu.SemaphoreType.DMA((2 + 3 * cuts,)),
+            pltpu.SemaphoreType.DMA((1 + 3 * cuts,)),
             pltpu.SemaphoreType.DMA((cuts,)),
         ],
+        limit=48,
     )
 
 
@@ -331,16 +336,15 @@
         weight_far,
         (near, base),
         (count,),
-        lax.axis_size("z"),
-    )
-    spread = whole(chip_sum.reshape(devices // 2, 2 * own_rows, depth // 2), ("z", "y", "x"))
+        tuple(lax.axis_size(axis) for axis in ("y", "x", "z")),
+    )
+    spread = whole(
+        chip_sum.reshape(devices, own_rows, depth // 2), ("core", "z", "x", "y")
+    )
     count = count + sum(across(count, step) for step in range(1, seq_devices))
-    summed = jnp.sum(spread.astype(F32), axis=0) * (float(rows * seq_devices) / count[0, 0])
-    first, second = summed[:own_rows], summed[own_rows:]
-    own = core == 0
-    keep = jnp.where(own, first, second).astype(BF16)
-    get = swap(jnp.where(own, second, first).astype(BF16))
-    hidden_grad = jnp.concatenate([jnp.where(own, keep, get), jnp.where(own, get, keep)], axis=1)
+    summed = jnp.sum(spread.astype(F32).reshape(2, devices // 2, own_rows, depth // 2), axis=1)
+    rounded = (summed * (float(rows * seq_devices) / count[0, 0])).astype(BF16)
+    hidden_grad = jnp.concatenate([rounded[0], rounded[1]], axis=1)
     return hidden_grad, token_kl
 
 

time: 102 us -> 98.2 us (0.963)
  waiting for transfers between devices: 27.6 us -> 26.2 us
    ppermute x4 -> x3, starting transfers between devices: 2.86 us -> 1.44 us  [swap(): return lax.ppermute(value, 'core', [(0, 1), (1, 0)])]
  transfers between devices with their start and end apart: 10 -> 9, of which waited for: 4 -> 3; matrix products, arithmetic and copies ran while one was open for 1% -> 1% of each run, Pallas kernels for 27% -> 28%
where the time goes in v5:
time: 98.2 us; the launch traced here: 97.8 us
  Pallas kernels  35.5 us (36%)
  starting transfers between devices  32.5 us (33%)
  waiting for transfers between devices  26.2 us (27%)
  other arithmetic  1.62 us (2%)
  between operations  1.46 us (1%)
    pallas_call x4, Pallas kernels, run(): pl.pallas_call(kernel, out_shape=outs, in_specs=specs, out_specs=out_spec...  35.5 us
    ppermute x3, waiting for transfers between devices, across(): lax.ppermute(value, 'seq', [(s, (s + step) % seq_devices) for s in range(...  20.8 us
    all_to_all x2, starting transfers between devices, whole(): return lax.all_to_all(value, axes, split_axis=0, concat_axis=0, tiled=True)  12.1 us
    all_to_all x1, starting transfers between devices, body(): lax.all_to_all(teacher_logprob, VOCAB, split_axis=1, concat_axis=0, tiled...  10.5 us
    ppermute x3, starting transfers between devices, across(): lax.ppermute(value, 'seq', [(s, (s + step) % seq_devices) for s in range(...  8.47 us
    all_to_all x1, waiting for transfers between devices, body(): lax.all_to_all(teacher_logprob, VOCAB, split_axis=1, concat_axis=0, tiled...  2.99 us
    all_to_all x2, waiting for transfers between devices, whole(): return lax.all_to_all(value, axes, split_axis=0, concat_axis=0, tiled=True)  2.44 us
  transfers between devices with their start and end apart: 9, of which 3 were waited for; matrix products, arithmetic and copies ran while one was open for 1% of the time, Pallas kernels for 28%

profile of v5, /device:TPU:1, one launch (start us, length us, event | category | flops | bytes accessed | tf_op | source)
XLA Modules:
  0.0 97.8 jit_solution(16181520438764279841)
XLA Ops:
  0.6 10.5 %all-to-all-start = ((bf16[8,64,1280]{2,0,1:T(8,128)(2,1)}), bf16[8,64,1280]{2,0,1:T(8,128)(2,1)}, u32[]{:S(2)}, u32[]{:S(2)}) async-start(bf16[8,64,1280]{2,0,1:T(8,128)(2,1)} %bitcast.16), calls=%async_computation | async-start | bytes 2621440 | tf_op jit(solution)/shard_map/all_to_all | solution.py:321
  11.2 0.6 collective-permute-start.2
  11.8 0.7 pad_add_fusion.where_ref
  12.4 16.6 %shard_map.59 = (f32[512,1408]{1,0:T(8,128)}, bf16[512,1280]{1,0:T(8,128)(2,1)}, bf16[512,2048]{1,0:T(8,128)(2,1)}, f32[8,128]{1,0:T(8,128)}) custom-call(s32[3]{0:T(128)} %pad_add_fusion.where_ref, s32[2]{0:T(128)} %lengths_ref.3, bf16[512,4096]{1,0:T(8,128)(2,1)} %hidden_ref.1, bf16[4096,1280]{1,0:T(8,128)(2,1)} %weight_ref.3), custom_call_target="tpu_custom_call" | custom-call | flops 199999995904 | tf_op jit(solution)/shard_map/pallas_call | solution.py:31
  29.1 0.1 collective-permute-start.1
  29.2 3.0 %all-to-all-done = bf16[8,64,1280]{2,0,1:T(8,128)(2,1)} async-done(((bf16[8,64,1280]{2,0,1:T(8,128)(2,1)}), bf16[8,64,1280]{2,0,1:T(8,128)(2,1)}, u32[]{:S(2)}, u32[]{:S(2)}) %all-to-all-start) | async-done | bytes 1310752 | tf_op jit(solution)/shard_map/all_to_all | solution.py:321
  32.2 4.3 %shard_map.60 = (bf16[512,1280]{1,0:T(8,128)(2,1)}, f32[64,2,512]{2,1,0:T(2,128)}) custom-call(f32[512,1408]{1,0:T(8,128)} %get-tuple-element.11.score_ref, bf16[512,1280]{1,0:T(8,128)(2,1)} %bitcast.5.teacher_ref), custom_call_target="tpu_custom_call" | custom-call | flops 49999998976 | tf_op jit(solution)/shard_map/pallas_call | solution.py:31
  36.5 5.8 %all-to-all-start.1 = ((f32[64,2,512]{2,1,0:T(2,128)}), f32[64,2,512]{2,1,0:T(2,128)S(1)}, u32[]{:S(2)}, u32[]{:S(2)}) async-start(f32[64,2,512]{2,1,0:T(2,128)} %get-tuple-element.12), calls=%async_computation.1 | async-start | bytes 524288 | tf_op jit(solution)/shard_map/all_to_all | solution.py:319
  42.4 0.0 copy-start
  42.4 0.0 copy-start.2
  42.4 0.7 collective-permute-start
  43.1 6.8 %shard_map.61.near_ref = bf16[512,2048]{1,0:T(8,128)(2,1)} custom-call(s32[3]{0:T(128)} %pad_add_fusion.where_ref, bf16[512,1280]{1,0:T(8,128)(2,1)} %get-tuple-element.13.left_ref, bf16[4096,1280]{1,0:T(8,128)(2,1)} %weight_ref.3), custom_call_target="tpu_custom_call" | custom-call | flops 49999998976 | tf_op jit(solution)/shard_map/pallas_call | solution.py:31
  49.9 0.0 collective-permute-done.1.probs_ref
  49.9 2.4 %all-to-all-done.1.stats_ref = f32[64,2,512]{2,1,0:T(2,128)S(1)} async-done(((f32[64,2,512]{2,1,0:T(2,128)}), f32[64,2,512]{2,1,0:T(2,128)S(1)}, u32[]{:S(2)}, u32[]{:S(2)}) %all-to-all-start.1) | async-done | bytes 262176 | tf_op jit(solution)/shard_map/all_to_all | solution.py:319
  52.4 0.0 collective-permute-done.grad_ref
  52.4 7.7 %shard_map.62 = (bf16[512,2048]{1,0:T(8,128)(2,1)}, f32[8]{0:T(128)}, f32[8,128]{1,0:T(8,128)S(1)}) custom-call(s32[3]{0:T(128)S(1)} %copy-done.1, s32[2]{0:T(128)S(1)} %copy-done.2, f32[64,2,512]{2,1,0:T(2,128)S(1)} %all-to-all-done.1.stats_ref, bf16[512,1280]{1,0:T(8,128)(2,1)} %collective-permute-done.grad_ref, ...), custom_call_target="tpu_custom_call" | custom-call | tf_op jit(solution)/shard_map/pallas_call | solution.py:31
  60.1 6.2 %all-to-all-start.2 = ((bf16[64,8,2048]{2,1,0:T(8,128)(2,1)}), bf16[64,8,2048]{2,1,0:T(8,128)(2,1)S(1)}, u32[]{:S(2)}, u32[]{:S(2)}) async-start(bf16[64,8,2048]{2,1,0:T(8,128)(2,1)} %bitcast.6), calls=%async_computation.2 | async-start | bytes 4194304 | tf_op jit(solution)/shard_map/all_to_all | solution.py:319
  66.4 5.2 %collective-permute-start.5 = (f32[8,128]{1,0:T(8,128)S(1)}, f32[8,128]{1,0:T(8,128)S(1)}, u32[]{:S(2)}, u32[]{:S(2)}) collective-permute-start(f32[8,128]{1,0:T(8,128)S(1)} %get-tuple-element.18), channel_id=1, source_target_pairs={{0,192},{64,0},{128,64},{192,128},{1,193},{65,1},{129,65},{193,129... | collective-permute-start | bytes 12296 | tf_op jit(solution)/shard_map/ppermute | solution.py:316
  71.6 1.2 %collective-permute-start.4 = (f32[8,128]{1,0:T(8,128)S(1)}, f32[8,128]{1,0:T(8,128)S(1)}, u32[]{:S(2)}, u32[]{:S(2)}) collective-permute-start(f32[8,128]{1,0:T(8,128)S(1)} %get-tuple-element.18), channel_id=1, source_target_pairs={{0,128},{64,192},{128,0},{192,64},{1,129},{65,193},{129,1},{193,65... | collective-permute-start | bytes 12296 | tf_op jit(solution)/shard_map/ppermute | solution.py:316
  72.8 2.1 %collective-permute-start.3 = (f32[8,128]{1,0:T(8,128)S(1)}, f32[8,128]{1,0:T(8,128)S(1)}, u32[]{:S(2)}, u32[]{:S(2)}) collective-permute-start(f32[8,128]{1,0:T(8,128)S(1)} %get-tuple-element.18), channel_id=1, source_target_pairs={{0,64},{64,128},{128,192},{192,0},{1,65},{65,129},{129,193},{193,1... | collective-permute-start | bytes 12296 | tf_op jit(solution)/shard_map/ppermute | solution.py:316
  74.9 20.8 %collective-permute-done.4 = f32[8,128]{1,0:T(8,128)S(1)} collective-permute-done((f32[8,128]{1,0:T(8,128)S(1)}, f32[8,128]{1,0:T(8,128)S(1)}, u32[]{:S(2)}, u32[]{:S(2)}) %collective-permute-start.4) | collective-permute-done | bytes 4128 | tf_op jit(solution)/shard_map/ppermute | solution.py:316
  95.6 0.5 slice.9
  96.9 0.3 convert_reduce_fusion
  97.2 0.6 pad_maximum_fusion
  (11 shorter events, 0.0 us)
Async XLA Ops:
  0.6 31.6 %all-to-all-start = ((bf16[8,64,1280]{2,0,1:T(8,128)(2,1)}), bf16[8,64,1280]{2,0,1:T(8,128)(2,1)}, u32[]{:S(2)}, u32[]{:S(2)}) async-start(bf16[8,64,1280]{2,0,1:T(8,128)(2,1)} %bitcast.16), calls=%async_computation | async-start | bytes 2621440 | tf_op jit(solution)/shard_map/all_to_all | solution.py:321
  11.2 41.2 %collective-permute-start.2 = (bf16[4096,1280]{1,0:T(8,128)(2,1)}, bf16[4096,1280]{1,0:T(8,128)(2,1)}, u32[]{:S(2)}, u32[]{:S(2)}) collective-permute-start(bf16[4096,1280]{1,0:T(8,128)(2,1)} %weight_ref.3), channel_id=1, source_target_pairs={{0,1},{1,0},{2,3},{3,2},{4,5},{5,4},{6,7},{7,6},{8,9},{9,8},{10,11... | collective-permute-start | bytes 31457288 | tf_op jit(solution)/shard_map/ppermute | solution.py:313
  29.1 20.8 %collective-permute-start.1 = (bf16[512,1280]{1,0:T(8,128)(2,1)}, bf16[512,1280]{1,0:T(8,128)(2,1)S(1)}, u32[]{:S(2)}, u32[]{:S(2)}) collective-permute-start(bf16[512,1280]{1,0:T(8,128)(2,1)} %get-tuple-element.14), channel_id=1, source_target_pairs={{0,1},{1,0},{2,3},{3,2},{4,5},{5,4},{6,7},{7,6},{8,9},{9,8},{10,11... | collective-permute-start | bytes 3932168 | tf_op jit(solution)/shard_map/ppermute | solution.py:313
  36.5 15.8 %all-to-all-start.1 = ((f32[64,2,512]{2,1,0:T(2,128)}), f32[64,2,512]{2,1,0:T(2,128)S(1)}, u32[]{:S(2)}, u32[]{:S(2)}) async-start(f32[64,2,512]{2,1,0:T(2,128)} %get-tuple-element.12), calls=%async_computation.1 | async-start | bytes 524288 | tf_op jit(solution)/shard_map/all_to_all | solution.py:319
  42.4 10.0 %copy-start = (f32[8,128]{1,0:T(8,128)S(1)}, f32[8,128]{1,0:T(8,128)}, u32[]{:S(2)}) copy-start(f32[8,128]{1,0:T(8,128)} %get-tuple-element.16.count_ref) | copy-start | bytes 12292
  42.4 10.0 %copy-start.1 = (s32[3]{0:T(128)S(1)}, s32[3]{0:T(128)}, u32[]{:S(2)}) copy-start(s32[3]{0:T(128)} %pad_add_fusion.where_ref) | copy-start | bytes 40
  42.4 10.0 %copy-start.2 = (s32[2]{0:T(128)S(1)}, s32[2]{0:T(128)}, u32[]{:S(2)}) copy-start(s32[2]{0:T(128)} %lengths_ref.3) | copy-start | bytes 28
  42.4 10.0 %collective-permute-start = (bf16[512,1280]{1,0:T(8,128)(2,1)}, bf16[512,1280]{1,0:T(8,128)(2,1)}, u32[]{:S(2)}, u32[]{:S(2)}) collective-permute-start(bf16[512,1280]{1,0:T(8,128)(2,1)} %get-tuple-element.13.left_ref), channel_id=1, source_target_pairs={{0,1},{1,0},{2,3},{3,2},{4,5},{5,4},{6,7},{7,6},{8,9},{9,8},{10,11... | collective-permute-start | bytes 3932168 | tf_op jit(solution)/shard_map/ppermute | solution.py:313
  60.1 36.7 %all-to-all-start.2 = ((bf16[64,8,2048]{2,1,0:T(8,128)(2,1)}), bf16[64,8,2048]{2,1,0:T(8,128)(2,1)S(1)}, u32[]{:S(2)}, u32[]{:S(2)}) async-start(bf16[64,8,2048]{2,1,0:T(8,128)(2,1)} %bitcast.6), calls=%async_computation.2 | async-start | bytes 4194304 | tf_op jit(solution)/shard_map/all_to_all | solution.py:319
  66.4 8.5 %collective-permute-start.5 = (f32[8,128]{1,0:T(8,128)S(1)}, f32[8,128]{1,0:T(8,128)S(1)}, u32[]{:S(2)}, u32[]{:S(2)}) collective-permute-start(f32[8,128]{1,0:T(8,128)S(1)} %get-tuple-element.18), channel_id=1, source_target_pairs={{0,192},{64,0},{128,64},{192,128},{1,193},{65,1},{129,65},{193,129... | collective-permute-start | bytes 12296 | tf_op jit(solution)/shard_map/ppermute | solution.py:316
  71.6 24.0 %collective-permute-start.4 = (f32[8,128]{1,0:T(8,128)S(1)}, f32[8,128]{1,0:T(8,128)S(1)}, u32[]{:S(2)}, u32[]{:S(2)}) collective-permute-start(f32[8,128]{1,0:T(8,128)S(1)} %get-tuple-element.18), channel_id=1, source_target_pairs={{0,128},{64,192},{128,0},{192,64},{1,129},{65,193},{129,1},{193,65... | collective-permute-start | bytes 12296 | tf_op jit(solution)/shard_map/ppermute | solution.py:316
  72.8 22.9 %collective-permute-start.3 = (f32[8,128]{1,0:T(8,128)S(1)}, f32[8,128]{1,0:T(8,128)S(1)}, u32[]{:S(2)}, u32[]{:S(2)}) collective-permute-start(f32[8,128]{1,0:T(8,128)S(1)} %get-tuple-element.18), channel_id=1, source_target_pairs={{0,64},{64,128},{128,192},{192,0},{1,65},{65,129},{129,193},{193,1... | collective-permute-start | bytes 12296 | tf_op jit(solution)/shard_map/ppermute | solution.py:316

commit v6 on v5

--- a/solution.py
+++ b/solution.py
@@ -249,7 +249,7 @@
         kl = jnp.broadcast_to(live * (level - lse), (8, rows))
         kl_ref[...] = pltpu.roll(kl, turn, 1)[0, :own_rows]
         lines = []
-        for k in (1, 2):
+        for k in (2, 3):
             stat = stats_ref[where_ref[k]]
             factor = live * jnp.exp(stat[0:1] - lse)
             lines += [factor, factor * (stat[1:2] - level)]
@@ -307,7 +307,10 @@
     seq_devices = lax.axis_size("seq")
     core = lax.axis_index("core").astype(jnp.int32)
     place = lax.axis_index(VOCAB).astype(jnp.int32)
-    where = jnp.stack([core, place, place + 1 - 2 * core])
+    order = ("core", "z", "x", "y")
+    spot = lax.axis_index(order).astype(jnp.int32)
+    sibling = spot + (1 - 2 * core) * (devices // 2)
+    where = jnp.stack([core, place, spot, sibling])
 
     def swap(value):
         return lax.ppermute(value, "core", [(0, 1), (1, 0)])
@@ -325,7 +328,7 @@
 
     grad, stats = middle(score, teacher, devices)
     grad_far = swap(grad)
-    stats = whole(stats, VOCAB)
+    stats = whole(stats, order)
     near = near_product(where, grad, head_weight)
 
     chip_sum, token_kl, count = chip_products(
@@ -339,11 +342,12 @@
         tuple(lax.axis_size(axis) for axis in ("y", "x", "z")),
     )
     spread = whole(
-        chip_sum.reshape(devices, own_rows, depth // 2), ("core", "z", "x", "y")
+        chip_sum.reshape(devices, own_rows, depth // 2), order
     )
     count = count + sum(across(count, step) for step in range(1, seq_devices))
     summed = jnp.sum(spread.astype(F32).reshape(2, devices // 2, own_rows, depth // 2), axis=1)
-    rounded = (summed * (float(rows * seq_devices) / count[0, 0])).astype(BF16)
+    weight = jnp.broadcast_to((float(rows * seq_devices) / count)[:own_rows, :1], summed.shape[1:])
+    rounded = (summed * weight[None]).astype(BF16)
     hidden_grad = jnp.concatenate([rounded[0], rounded[1]], axis=1)
     return hidden_grad, token_kl
 

time: 98.2 us -> 97.2 us (0.990)
  transfers between devices with their start and end apart: 9 -> 9, of which waited for: 3 -> 3; matrix products, arithmetic and copies ran while one was open for 1% -> 1% of each run, Pallas kernels for 28% -> 29%
where the time goes in v6:
time: 97.2 us; the launch traced here: 96.8 us
  Pallas kernels  35.5 us (37%)
  starting transfers between devices  32.5 us (33%)
  waiting for transfers between devices  26.2 us (27%)
  other arithmetic  1.64 us (2%)
    pallas_call x4, Pallas kernels, run(): pl.pallas_call(kernel, out_shape=outs, in_specs=specs, out_specs=out_spec...  35.5 us
    ppermute x3, waiting for transfers between devices, across(): lax.ppermute(value, 'seq', [(s, (s + step) % seq_devices) for s in range(...  20.8 us
    all_to_all x2, starting transfers between devices, whole(): return lax.all_to_all(value, axes, split_axis=0, concat_axis=0, tiled=True)  12.2 us
    all_to_all x1, starting transfers between devices, body(): lax.all_to_all(teacher_logprob, VOCAB, split_axis=1, concat_axis=0, tiled...  10.5 us
    ppermute x3, starting transfers between devices, across(): lax.ppermute(value, 'seq', [(s, (s + step) % seq_devices) for s in range(...  8.46 us
    all_to_all x1, waiting for transfers between devices, body(): lax.all_to_all(teacher_logprob, VOCAB, split_axis=1, concat_axis=0, tiled...  3.06 us
    all_to_all x2, waiting for transfers between devices, whole(): return lax.all_to_all(value, axes, split_axis=0, concat_axis=0, tiled=True)  2.39 us
  transfers between devices with their start and end apart: 9, of which 3 were waited for; matrix products, arithmetic and copies ran while one was open for 1% of the time, Pallas kernels for 29%

profile of v6, /device:TPU:1, one launch (start us, length us, event | category | flops | bytes accessed | tf_op | source)
XLA Modules:
  0.0 96.8 jit_solution(5293099835896228022)
XLA Ops:
  0.6 10.5 %all-to-all-start = ((bf16[8,64,1280]{2,0,1:T(8,128)(2,1)}), bf16[8,64,1280]{2,0,1:T(8,128)(2,1)}, u32[]{:S(2)}, u32[]{:S(2)}) async-start(bf16[8,64,1280]{2,0,1:T(8,128)(2,1)} %bitcast.16), calls=%async_computation | async-start | bytes 2621440 | tf_op jit(solution)/shard_map/all_to_all | solution.py:324
  11.2 0.6 collective-permute-start.2
  11.8 0.6 pad_add_fusion.where_ref
  12.4 16.6 %shard_map.59 = (f32[512,1408]{1,0:T(8,128)}, bf16[512,1280]{1,0:T(8,128)(2,1)}, bf16[512,2048]{1,0:T(8,128)(2,1)}, f32[8,128]{1,0:T(8,128)}) custom-call(s32[4]{0:T(128)} %pad_add_fusion.where_ref, s32[2]{0:T(128)} %lengths_ref.3, bf16[512,4096]{1,0:T(8,128)(2,1)} %hidden_ref.1, bf16[4096,1280]{1,0:T(8,128)(2,1)} %weight_ref.3), custom_call_target="tpu_custom_call" | custom-call | flops 199999995904 | tf_op jit(solution)/shard_map/pallas_call | solution.py:31
  29.0 0.1 collective-permute-start.1
  29.1 3.1 %all-to-all-done = bf16[8,64,1280]{2,0,1:T(8,128)(2,1)} async-done(((bf16[8,64,1280]{2,0,1:T(8,128)(2,1)}), bf16[8,64,1280]{2,0,1:T(8,128)(2,1)}, u32[]{:S(2)}, u32[]{:S(2)}) %all-to-all-start) | async-done | bytes 1310752 | tf_op jit(solution)/shard_map/all_to_all | solution.py:324
  32.2 4.4 %shard_map.60 = (bf16[512,1280]{1,0:T(8,128)(2,1)}, f32[64,2,512]{2,1,0:T(2,128)}) custom-call(f32[512,1408]{1,0:T(8,128)} %get-tuple-element.11.score_ref, bf16[512,1280]{1,0:T(8,128)(2,1)} %bitcast.6.teacher_ref), custom_call_target="tpu_custom_call" | custom-call | flops 49999998976 | tf_op jit(solution)/shard_map/pallas_call | solution.py:31
  36.6 5.8 %all-to-all-start.1 = ((f32[64,2,512]{2,1,0:T(2,128)}), f32[64,2,512]{2,1,0:T(2,128)S(1)}, u32[]{:S(2)}, u32[]{:S(2)}) async-start(f32[64,2,512]{2,1,0:T(2,128)} %get-tuple-element.12), calls=%async_computation.1 | async-start | bytes 524288 | tf_op jit(solution)/shard_map/all_to_all | solution.py:322
  42.4 0.0 copy-start
  42.4 0.0 copy-start.2
  42.4 0.6 collective-permute-start
  43.1 6.8 %shard_map.61.near_ref = bf16[512,2048]{1,0:T(8,128)(2,1)} custom-call(s32[4]{0:T(128)} %pad_add_fusion.where_ref, bf16[512,1280]{1,0:T(8,128)(2,1)} %get-tuple-element.13.left_ref, bf16[4096,1280]{1,0:T(8,128)(2,1)} %weight_ref.3), custom_call_target="tpu_custom_call" | custom-call | flops 49999998976 | tf_op jit(solution)/shard_map/pallas_call | solution.py:31
  49.9 2.4 %all-to-all-done.1.stats_ref = f32[64,2,512]{2,1,0:T(2,128)S(1)} async-done(((f32[64,2,512]{2,1,0:T(2,128)}), f32[64,2,512]{2,1,0:T(2,128)S(1)}, u32[]{:S(2)}, u32[]{:S(2)}) %all-to-all-start.1) | async-done | bytes 262176 | tf_op jit(solution)/shard_map/all_to_all | solution.py:322
  52.3 0.0 collective-permute-done.grad_ref
  52.3 7.7 %shard_map.62 = (bf16[512,2048]{1,0:T(8,128)(2,1)}, f32[8]{0:T(128)}, f32[8,128]{1,0:T(8,128)S(1)}) custom-call(s32[4]{0:T(128)S(1)} %copy-done.1, s32[2]{0:T(128)S(1)} %copy-done.2, f32[64,2,512]{2,1,0:T(2,128)S(1)} %all-to-all-done.1.stats_ref, bf16[512,1280]{1,0:T(8,128)(2,1)} %collective-permute-done.grad_ref, ...), custom_call_target="tpu_custom_call" | custom-call | tf_op jit(solution)/shard_map/pallas_call | solution.py:31
  60.0 6.3 %all-to-all-start.2 = ((bf16[64,8,2048]{2,1,0:T(8,128)(2,1)}), bf16[64,8,2048]{2,1,0:T(8,128)(2,1)S(1)}, u32[]{:S(2)}, u32[]{:S(2)}) async-start(bf16[64,8,2048]{2,1,0:T(8,128)(2,1)} %bitcast.7), calls=%async_computation.2 | async-start | bytes 4194304 | tf_op jit(solution)/shard_map/all_to_all | solution.py:322
  66.4 5.2 %collective-permute-start.5 = (f32[8,128]{1,0:T(8,128)S(1)}, f32[8,128]{1,0:T(8,128)S(1)}, u32[]{:S(2)}, u32[]{:S(2)}) collective-permute-start(f32[8,128]{1,0:T(8,128)S(1)} %get-tuple-element.18), channel_id=1, source_target_pairs={{0,192},{64,0},{128,64},{192,128},{1,193},{65,1},{129,65},{193,129... | collective-permute-start | bytes 12296 | tf_op jit(solution)/shard_map/ppermute | solution.py:319
  71.6 1.2 %collective-permute-start.4 = (f32[8,128]{1,0:T(8,128)S(1)}, f32[8,128]{1,0:T(8,128)S(1)}, u32[]{:S(2)}, u32[]{:S(2)}) collective-permute-start(f32[8,128]{1,0:T(8,128)S(1)} %get-tuple-element.18), channel_id=1, source_target_pairs={{0,128},{64,192},{128,0},{192,64},{1,129},{65,193},{129,1},{193,65... | collective-permute-start | bytes 12296 | tf_op jit(solution)/shard_map/ppermute | solution.py:319
  72.8 2.1 %collective-permute-start.3 = (f32[8,128]{1,0:T(8,128)S(1)}, f32[8,128]{1,0:T(8,128)S(1)}, u32[]{:S(2)}, u32[]{:S(2)}) collective-permute-start(f32[8,128]{1,0:T(8,128)S(1)} %get-tuple-element.18), channel_id=1, source_target_pairs={{0,64},{64,128},{128,192},{192,0},{1,65},{65,129},{129,193},{193,1... | collective-permute-start | bytes 12296 | tf_op jit(solution)/shard_map/ppermute | solution.py:319
  74.9 20.7 %collective-permute-done.4 = f32[8,128]{1,0:T(8,128)S(1)} collective-permute-done((f32[8,128]{1,0:T(8,128)S(1)}, f32[8,128]{1,0:T(8,128)S(1)}, u32[]{:S(2)}, u32[]{:S(2)}) %collective-permute-start.4) | collective-permute-done | bytes 4128 | tf_op jit(solution)/shard_map/ppermute | solution.py:319
  95.6 0.1 slice_reduce_fusion
  95.8 0.3 convert_reduce_fusion
  96.1 0.1 multiply_convert_fusion
  96.1 0.6 pad_maximum_fusion
  (11 shorter events, 0.0 us)
Async XLA Ops:
  0.6 31.6 %all-to-all-start = ((bf16[8,64,1280]{2,0,1:T(8,128)(2,1)}), bf16[8,64,1280]{2,0,1:T(8,128)(2,1)}, u32[]{:S(2)}, u32[]{:S(2)}) async-start(bf16[8,64,1280]{2,0,1:T(8,128)(2,1)} %bitcast.16), calls=%async_computation | async-start | bytes 2621440 | tf_op jit(solution)/shard_map/all_to_all | solution.py:324
  11.2 41.1 %collective-permute-start.2 = (bf16[4096,1280]{1,0:T(8,128)(2,1)}, bf16[4096,1280]{1,0:T(8,128)(2,1)}, u32[]{:S(2)}, u32[]{:S(2)}) collective-permute-start(bf16[4096,1280]{1,0:T(8,128)(2,1)} %weight_ref.3), channel_id=1, source_target_pairs={{0,1},{1,0},{2,3},{3,2},{4,5},{5,4},{6,7},{7,6},{8,9},{9,8},{10,11... | collective-permute-start | bytes 31457288 | tf_op jit(solution)/shard_map/ppermute | solution.py:316
  29.0 20.8 %collective-permute-start.1 = (bf16[512,1280]{1,0:T(8,128)(2,1)}, bf16[512,1280]{1,0:T(8,128)(2,1)S(1)}, u32[]{:S(2)}, u32[]{:S(2)}) collective-permute-start(bf16[512,1280]{1,0:T(8,128)(2,1)} %get-tuple-element.14), channel_id=1, source_target_pairs={{0,1},{1,0},{2,3},{3,2},{4,5},{5,4},{6,7},{7,6},{8,9},{9,8},{10,11... | collective-permute-start | bytes 3932168 | tf_op jit(solution)/shard_map/ppermute | solution.py:316
  36.6 15.7 %all-to-all-start.1 = ((f32[64,2,512]{2,1,0:T(2,128)}), f32[64,2,512]{2,1,0:T(2,128)S(1)}, u32[]{:S(2)}, u32[]{:S(2)}) async-start(f32[64,2,512]{2,1,0:T(2,128)} %get-tuple-element.12), calls=%async_computation.1 | async-start | bytes 524288 | tf_op jit(solution)/shard_map/all_to_all | solution.py:322
  42.4 9.9 %copy-start = (f32[8,128]{1,0:T(8,128)S(1)}, f32[8,128]{1,0:T(8,128)}, u32[]{:S(2)}) copy-start(f32[8,128]{1,0:T(8,128)} %get-tuple-element.16.count_ref) | copy-start | bytes 12292
  42.4 9.9 %copy-start.1 = (s32[4]{0:T(128)S(1)}, s32[4]{0:T(128)}, u32[]{:S(2)}) copy-start(s32[4]{0:T(128)} %pad_add_fusion.where_ref) | copy-start | bytes 52
  42.4 9.9 %copy-start.2 = (s32[2]{0:T(128)S(1)}, s32[2]{0:T(128)}, u32[]{:S(2)}) copy-start(s32[2]{0:T(128)} %lengths_ref.3) | copy-start | bytes 28
  42.4 9.8 %collective-permute-start = (bf16[512,1280]{1,0:T(8,128)(2,1)}, bf16[512,1280]{1,0:T(8,128)(2,1)}, u32[]{:S(2)}, u32[]{:S(2)}) collective-permute-start(bf16[512,1280]{1,0:T(8,128)(2,1)} %get-tuple-element.13.left_ref), channel_id=1, source_target_pairs={{0,1},{1,0},{2,3},{3,2},{4,5},{5,4},{6,7},{7,6},{8,9},{9,8},{10,11... | collective-permute-start | bytes 3932168 | tf_op jit(solution)/shard_map/ppermute | solution.py:316
  60.0 35.7 %all-to-all-start.2 = ((bf16[64,8,2048]{2,1,0:T(8,128)(2,1)}), bf16[64,8,2048]{2,1,0:T(8,128)(2,1)S(1)}, u32[]{:S(2)}, u32[]{:S(2)}) async-start(bf16[64,8,2048]{2,1,0:T(8,128)(2,1)} %bitcast.7), calls=%async_computation.2 | async-start | bytes 4194304 | tf_op jit(solution)/shard_map/all_to_all | solution.py:322
  66.4 8.5 %collective-permute-start.5 = (f32[8,128]{1,0:T(8,128)S(1)}, f32[8,128]{1,0:T(8,128)S(1)}, u32[]{:S(2)}, u32[]{:S(2)}) collective-permute-start(f32[8,128]{1,0:T(8,128)S(1)} %get-tuple-element.18), channel_id=1, source_target_pairs={{0,192},{64,0},{128,64},{192,128},{1,193},{65,1},{129,65},{193,129... | collective-permute-start | bytes 12296 | tf_op jit(solution)/shard_map/ppermute | solution.py:319
  71.6 24.0 %collective-permute-start.4 = (f32[8,128]{1,0:T(8,128)S(1)}, f32[8,128]{1,0:T(8,128)S(1)}, u32[]{:S(2)}, u32[]{:S(2)}) collective-permute-start(f32[8,128]{1,0:T(8,128)S(1)} %get-tuple-element.18), channel_id=1, source_target_pairs={{0,128},{64,192},{128,0},{192,64},{1,129},{65,193},{129,1},{193,65... | collective-permute-start | bytes 12296 | tf_op jit(solution)/shard_map/ppermute | solution.py:319
  72.8 22.8 %collective-permute-start.3 = (f32[8,128]{1,0:T(8,128)S(1)}, f32[8,128]{1,0:T(8,128)S(1)}, u32[]{:S(2)}, u32[]{:S(2)}) collective-permute-start(f32[8,128]{1,0:T(8,128)S(1)} %get-tuple-element.18), channel_id=1, source_target_pairs={{0,64},{64,128},{128,192},{192,0},{1,65},{65,129},{129,193},{193,1... | collective-permute-start | bytes 12296 | tf_op jit(solution)/shard_map/ppermute | solution.py:319

commit v7 on v6

--- a/solution.py
+++ b/solution.py
@@ -176,21 +176,34 @@
     rows, width = teacher.shape
 
     def kernel(score_ref, teacher_ref, grad_ref, stats_ref, held, target, grad, lines, sems):
-        copies = moves([(score_ref, held), (teacher_ref, target)], sems)
-        for copy in copies:
-            copy.wait()
-        score = held[:, pl.ds(0, width)]
-        probs = jnp.exp(score)
-        advantage = score - target[...].astype(F32)
-        mean = jnp.sum(probs * advantage, axis=1, keepdims=True)
-        lse = held[:, pl.ds(width, LANES)][:, 0:1]
-        block = packed((lse, mean + lse), rows).T[:2]
+        parts = 2
+        part = rows // parts
+        copies = moves(
+            [
+                (a.at[pl.ds(k * part, part), :], b.at[pl.ds(k * part, part), :])
+                for k in range(parts)
+                for a, b in ((score_ref, held), (teacher_ref, target))
+            ],
+            sems,
+        )
+        blocks, means = [], []
+        for k in range(parts):
+            at = pl.ds(k * part, part)
+            copies[2 * k].wait()
+            copies[2 * k + 1].wait()
+            score = held[at, pl.ds(0, width)]
+            probs = jnp.exp(score)
+            advantage = score - target[at, :].astype(F32)
+            mean = jnp.sum(probs * advantage, axis=1, keepdims=True)
+            lse = held[at, pl.ds(width, LANES)][:, 0:1]
+            blocks.append(packed((lse, mean + lse), part).T[:2])
+            grad[at, :] = (probs * (advantage - mean)).astype(BF16)
+        block = jnp.concatenate(blocks, axis=1)
         for k in range(devices):
             lines[k] = block
-        stats_copy = pltpu.make_async_copy(lines, stats_ref, sems.at[2])
+        stats_copy = pltpu.make_async_copy(lines, stats_ref, sems.at[2 * parts])
         stats_copy.start()
-        grad[...] = (probs * (advantage - mean)).astype(BF16)
-        grad_copy = pltpu.make_async_copy(grad, grad_ref, sems.at[3])
+        grad_copy = pltpu.make_async_copy(grad, grad_ref, sems.at[2 * parts + 1])
         grad_copy.start()
         stats_copy.wait()
         grad_copy.wait()
@@ -206,7 +219,7 @@
             pltpu.VMEM((rows, width), BF16),
             pltpu.VMEM((rows, width), BF16),
             pltpu.VMEM((devices, 2, rows), F32),
-            pltpu.SemaphoreType.DMA((4,)),
+            pltpu.SemaphoreType.DMA((6,)),
         ],
         flops=50 * 10**9,
     )

time: 97.2 us -> 96.7 us (level)
  transfers between devices with their start and end apart: 9 -> 9, of which waited for: 3 -> 3; matrix products, arithmetic and copies ran while one was open for 1% -> 1% of each run, Pallas kernels for 29% -> 28%
where the time goes in v7:
time: 96.7 us; the launch traced here: 96.3 us
  Pallas kernels  35 us (36%)
  starting transfers between devices  32.5 us (34%)
  waiting for transfers between devices  26.2 us (27%)
  other arithmetic  1.64 us (2%)
    pallas_call x4, Pallas kernels, run(): pl.pallas_call(kernel, out_shape=outs, in_specs=specs, out_specs=out_spec...  35 us
    ppermute x3, waiting for transfers between devices, across(): lax.ppermute(value, 'seq', [(s, (s + step) % seq_devices) for s in range(...  20.8 us
    all_to_all x2, starting transfers between devices, whole(): return lax.all_to_all(value, axes, split_axis=0, concat_axis=0, tiled=True)  12.2 us
    all_to_all x1, starting transfers between devices, body(): lax.all_to_all(teacher_logprob, VOCAB, split_axis=1, concat_axis=0, tiled...  10.5 us
    ppermute x3, starting transfers between devices, across(): lax.ppermute(value, 'seq', [(s, (s + step) % seq_devices) for s in range(...  8.44 us
    all_to_all x1, waiting for transfers between devices, body(): lax.all_to_all(teacher_logprob, VOCAB, split_axis=1, concat_axis=0, tiled...  3.06 us
    all_to_all x2, waiting for transfers between devices, whole(): return lax.all_to_all(value, axes, split_axis=0, concat_axis=0, tiled=True)  2.39 us
  transfers between devices with their start and end apart: 9, of which 3 were waited for; matrix products, arithmetic and copies ran while one was open for 1% of the time, Pallas kernels for 28%

profile of v7, /device:TPU:1, one launch (start us, length us, event | category | flops | bytes accessed | tf_op | source)
XLA Modules:
  0.0 96.3 jit_solution(10017703092530464443)
XLA Ops:
  0.6 10.5 %all-to-all-start = ((bf16[8,64,1280]{2,0,1:T(8,128)(2,1)}), bf16[8,64,1280]{2,0,1:T(8,128)(2,1)}, u32[]{:S(2)}, u32[]{:S(2)}) async-start(bf16[8,64,1280]{2,0,1:T(8,128)(2,1)} %bitcast.16), calls=%async_computation | async-start | bytes 2621440 | tf_op jit(solution)/shard_map/all_to_all | solution.py:337
  11.2 0.6 collective-permute-start.2
  11.8 0.6 pad_add_fusion.where_ref
  12.4 16.6 %shard_map.59 = (f32[512,1408]{1,0:T(8,128)}, bf16[512,1280]{1,0:T(8,128)(2,1)}, bf16[512,2048]{1,0:T(8,128)(2,1)}, f32[8,128]{1,0:T(8,128)}) custom-call(s32[4]{0:T(128)} %pad_add_fusion.where_ref, s32[2]{0:T(128)} %lengths_ref.3, bf16[512,4096]{1,0:T(8,128)(2,1)} %hidden_ref.1, bf16[4096,1280]{1,0:T(8,128)(2,1)} %weight_ref.3), custom_call_target="tpu_custom_call" | custom-call | flops 199999995904 | tf_op jit(solution)/shard_map/pallas_call | solution.py:31
  29.0 0.1 collective-permute-start.1
  29.1 3.1 %all-to-all-done = bf16[8,64,1280]{2,0,1:T(8,128)(2,1)} async-done(((bf16[8,64,1280]{2,0,1:T(8,128)(2,1)}), bf16[8,64,1280]{2,0,1:T(8,128)(2,1)}, u32[]{:S(2)}, u32[]{:S(2)}) %all-to-all-start) | async-done | bytes 1310752 | tf_op jit(solution)/shard_map/all_to_all | solution.py:337
  32.2 3.9 %shard_map.60 = (bf16[512,1280]{1,0:T(8,128)(2,1)}, f32[64,2,512]{2,1,0:T(2,128)}) custom-call(f32[512,1408]{1,0:T(8,128)} %get-tuple-element.11.score_ref, bf16[512,1280]{1,0:T(8,128)(2,1)} %bitcast.6.teacher_ref), custom_call_target="tpu_custom_call" | custom-call | flops 49999998976 | tf_op jit(solution)/shard_map/pallas_call | solution.py:31
  36.1 5.8 %all-to-all-start.1 = ((f32[64,2,512]{2,1,0:T(2,128)}), f32[64,2,512]{2,1,0:T(2,128)S(1)}, u32[]{:S(2)}, u32[]{:S(2)}) async-start(f32[64,2,512]{2,1,0:T(2,128)} %get-tuple-element.12), calls=%async_computation.1 | async-start | bytes 524288 | tf_op jit(solution)/shard_map/all_to_all | solution.py:335
  41.9 0.0 copy-start
  42.0 0.0 copy-start.2
  42.0 0.6 collective-permute-start
  42.6 6.8 %shard_map.61.near_ref = bf16[512,2048]{1,0:T(8,128)(2,1)} custom-call(s32[4]{0:T(128)} %pad_add_fusion.where_ref, bf16[512,1280]{1,0:T(8,128)(2,1)} %get-tuple-element.13.left_ref, bf16[4096,1280]{1,0:T(8,128)(2,1)} %weight_ref.3), custom_call_target="tpu_custom_call" | custom-call | flops 49999998976 | tf_op jit(solution)/shard_map/pallas_call | solution.py:31
  49.4 0.0 collective-permute-done.1.probs_ref
  49.4 2.4 %all-to-all-done.1.stats_ref = f32[64,2,512]{2,1,0:T(2,128)S(1)} async-done(((f32[64,2,512]{2,1,0:T(2,128)}), f32[64,2,512]{2,1,0:T(2,128)S(1)}, u32[]{:S(2)}, u32[]{:S(2)}) %all-to-all-start.1) | async-done | bytes 262176 | tf_op jit(solution)/shard_map/all_to_all | solution.py:335
  51.8 7.7 %shard_map.62 = (bf16[512,2048]{1,0:T(8,128)(2,1)}, f32[8]{0:T(128)}, f32[8,128]{1,0:T(8,128)S(1)}) custom-call(s32[4]{0:T(128)S(1)} %copy-done.1, s32[2]{0:T(128)S(1)} %copy-done.2, f32[64,2,512]{2,1,0:T(2,128)S(1)} %all-to-all-done.1.stats_ref, bf16[512,1280]{1,0:T(8,128)(2,1)} %collective-permute-done.grad_ref, ...), custom_call_target="tpu_custom_call" | custom-call | tf_op jit(solution)/shard_map/pallas_call | solution.py:31
  59.6 6.4 %all-to-all-start.2 = ((bf16[64,8,2048]{2,1,0:T(8,128)(2,1)}), bf16[64,8,2048]{2,1,0:T(8,128)(2,1)S(1)}, u32[]{:S(2)}, u32[]{:S(2)}) async-start(bf16[64,8,2048]{2,1,0:T(8,128)(2,1)} %bitcast.7), calls=%async_computation.2 | async-start | bytes 4194304 | tf_op jit(solution)/shard_map/all_to_all | solution.py:335
  65.9 5.2 %collective-permute-start.5 = (f32[8,128]{1,0:T(8,128)S(1)}, f32[8,128]{1,0:T(8,128)S(1)}, u32[]{:S(2)}, u32[]{:S(2)}) collective-permute-start(f32[8,128]{1,0:T(8,128)S(1)} %get-tuple-element.18), channel_id=1, source_target_pairs={{0,192},{64,0},{128,64},{192,128},{1,193},{65,1},{129,65},{193,129... | collective-permute-start | bytes 12296 | tf_op jit(solution)/shard_map/ppermute | solution.py:332
  71.1 1.2 %collective-permute-start.4 = (f32[8,128]{1,0:T(8,128)S(1)}, f32[8,128]{1,0:T(8,128)S(1)}, u32[]{:S(2)}, u32[]{:S(2)}) collective-permute-start(f32[8,128]{1,0:T(8,128)S(1)} %get-tuple-element.18), channel_id=1, source_target_pairs={{0,128},{64,192},{128,0},{192,64},{1,129},{65,193},{129,1},{193,65... | collective-permute-start | bytes 12296 | tf_op jit(solution)/shard_map/ppermute | solution.py:332
  72.3 2.1 %collective-permute-start.3 = (f32[8,128]{1,0:T(8,128)S(1)}, f32[8,128]{1,0:T(8,128)S(1)}, u32[]{:S(2)}, u32[]{:S(2)}) collective-permute-start(f32[8,128]{1,0:T(8,128)S(1)} %get-tuple-element.18), channel_id=1, source_target_pairs={{0,64},{64,128},{128,192},{192,0},{1,65},{65,129},{129,193},{193,1... | collective-permute-start | bytes 12296 | tf_op jit(solution)/shard_map/ppermute | solution.py:332
  74.4 20.7 %collective-permute-done.4 = f32[8,128]{1,0:T(8,128)S(1)} collective-permute-done((f32[8,128]{1,0:T(8,128)S(1)}, f32[8,128]{1,0:T(8,128)S(1)}, u32[]{:S(2)}, u32[]{:S(2)}) %collective-permute-start.4) | collective-permute-done | bytes 4128 | tf_op jit(solution)/shard_map/ppermute | solution.py:332
  95.1 0.1 slice_reduce_fusion
  95.3 0.3 convert_reduce_fusion
  95.6 0.1 multiply_convert_fusion
  95.7 0.6 pad_maximum_fusion
  (11 shorter events, 0.0 us)
Async XLA Ops:
  0.6 31.6 %all-to-all-start = ((bf16[8,64,1280]{2,0,1:T(8,128)(2,1)}), bf16[8,64,1280]{2,0,1:T(8,128)(2,1)}, u32[]{:S(2)}, u32[]{:S(2)}) async-start(bf16[8,64,1280]{2,0,1:T(8,128)(2,1)} %bitcast.16), calls=%async_computation | async-start | bytes 2621440 | tf_op jit(solution)/shard_map/all_to_all | solution.py:337
  11.2 40.6 %collective-permute-start.2 = (bf16[4096,1280]{1,0:T(8,128)(2,1)}, bf16[4096,1280]{1,0:T(8,128)(2,1)}, u32[]{:S(2)}, u32[]{:S(2)}) collective-permute-start(bf16[4096,1280]{1,0:T(8,128)(2,1)} %weight_ref.3), channel_id=1, source_target_pairs={{0,1},{1,0},{2,3},{3,2},{4,5},{5,4},{6,7},{7,6},{8,9},{9,8},{10,11... | collective-permute-start | bytes 31457288 | tf_op jit(solution)/shard_map/ppermute | solution.py:329
  29.0 20.4 %collective-permute-start.1 = (bf16[512,1280]{1,0:T(8,128)(2,1)}, bf16[512,1280]{1,0:T(8,128)(2,1)S(1)}, u32[]{:S(2)}, u32[]{:S(2)}) collective-permute-start(bf16[512,1280]{1,0:T(8,128)(2,1)} %get-tuple-element.14), channel_id=1, source_target_pairs={{0,1},{1,0},{2,3},{3,2},{4,5},{5,4},{6,7},{7,6},{8,9},{9,8},{10,11... | collective-permute-start | bytes 3932168 | tf_op jit(solution)/shard_map/ppermute | solution.py:329
  36.1 15.7 %all-to-all-start.1 = ((f32[64,2,512]{2,1,0:T(2,128)}), f32[64,2,512]{2,1,0:T(2,128)S(1)}, u32[]{:S(2)}, u32[]{:S(2)}) async-start(f32[64,2,512]{2,1,0:T(2,128)} %get-tuple-element.12), calls=%async_computation.1 | async-start | bytes 524288 | tf_op jit(solution)/shard_map/all_to_all | solution.py:335
  41.9 9.9 %copy-start = (f32[8,128]{1,0:T(8,128)S(1)}, f32[8,128]{1,0:T(8,128)}, u32[]{:S(2)}) copy-start(f32[8,128]{1,0:T(8,128)} %get-tuple-element.16.count_ref) | copy-start | bytes 12292
  41.9 9.9 %copy-start.1 = (s32[4]{0:T(128)S(1)}, s32[4]{0:T(128)}, u32[]{:S(2)}) copy-start(s32[4]{0:T(128)} %pad_add_fusion.where_ref) | copy-start | bytes 52
  42.0 9.9 %copy-start.2 = (s32[2]{0:T(128)S(1)}, s32[2]{0:T(128)}, u32[]{:S(2)}) copy-start(s32[2]{0:T(128)} %lengths_ref.3) | copy-start | bytes 28
  42.0 9.8 %collective-permute-start = (bf16[512,1280]{1,0:T(8,128)(2,1)}, bf16[512,1280]{1,0:T(8,128)(2,1)}, u32[]{:S(2)}, u32[]{:S(2)}) collective-permute-start(bf16[512,1280]{1,0:T(8,128)(2,1)} %get-tuple-element.13.left_ref), channel_id=1, source_target_pairs={{0,1},{1,0},{2,3},{3,2},{4,5},{5,4},{6,7},{7,6},{8,9},{9,8},{10,11... | collective-permute-start | bytes 3932168 | tf_op jit(solution)/shard_map/ppermute | solution.py:329
  59.6 35.7 %all-to-all-start.2 = ((bf16[64,8,2048]{2,1,0:T(8,128)(2,1)}), bf16[64,8,2048]{2,1,0:T(8,128)(2,1)S(1)}, u32[]{:S(2)}, u32[]{:S(2)}) async-start(bf16[64,8,2048]{2,1,0:T(8,128)(2,1)} %bitcast.7), calls=%async_computation.2 | async-start | bytes 4194304 | tf_op jit(solution)/shard_map/all_to_all | solution.py:335
  65.9 8.4 %collective-permute-start.5 = (f32[8,128]{1,0:T(8,128)S(1)}, f32[8,128]{1,0:T(8,128)S(1)}, u32[]{:S(2)}, u32[]{:S(2)}) collective-permute-start(f32[8,128]{1,0:T(8,128)S(1)} %get-tuple-element.18), channel_id=1, source_target_pairs={{0,192},{64,0},{128,64},{192,128},{1,193},{65,1},{129,65},{193,129... | collective-permute-start | bytes 12296 | tf_op jit(solution)/shard_map/ppermute | solution.py:332
  71.1 24.0 %collective-permute-start.4 = (f32[8,128]{1,0:T(8,128)S(1)}, f32[8,128]{1,0:T(8,128)S(1)}, u32[]{:S(2)}, u32[]{:S(2)}) collective-permute-start(f32[8,128]{1,0:T(8,128)S(1)} %get-tuple-element.18), channel_id=1, source_target_pairs={{0,128},{64,192},{128,0},{192,64},{1,129},{65,193},{129,1},{193,65... | collective-permute-start | bytes 12296 | tf_op jit(solution)/shard_map/ppermute | solution.py:332
  72.3 22.8 %collective-permute-start.3 = (f32[8,128]{1,0:T(8,128)S(1)}, f32[8,128]{1,0:T(8,128)S(1)}, u32[]{:S(2)}, u32[]{:S(2)}) collective-permute-start(f32[8,128]{1,0:T(8,128)S(1)} %get-tuple-element.18), channel_id=1, source_target_pairs={{0,64},{64,128},{128,192},{192,0},{1,65},{65,129},{129,193},{193,1... | collective-permute-start | bytes 12296 | tf_op jit(solution)/shard_map/ppermute | solution.py:332
